TPU v7x, 128 devices: a whole 4x4x4 slice. The times are simulated.
128 devices in a mesh: lat: 8 (over y, z_hi), lon: 16 (over x, z_lo, core).
Axes of the slice: x: 4, y: 4, z: 4 (z_hi: 2, z_lo: 2; z = z_hi * 2 + z_lo), core: 2. Of those that a mesh axis runs over, the one named last changes fastest.
Arguments:
- tokens: bfloat16 [4, 48, 768, 512], P(None, 'lat', 'lon'), may hold values from -36 to 36
- band_ids: int32 [48], replicated, may hold values from 0 to 23, never falling along the last dimension, each value on 1 to 4 neighbouring positions
- qkv_weight: bfloat16 [512, 1536], replicated, may hold values from -16 to 16
- proj_weight: bfloat16 [512, 512], replicated, may hold values from -0.25 to 0.25
- fc1_weight: bfloat16 [512, 2048], replicated, may hold values from -0.25 to 0.25
- fc2_weight: bfloat16 [2048, 512], replicated, may hold values from -0.125 to 0.125
- merge_weight: bfloat16 [2048, 1024], replicated, may hold values from -0.125 to 0.125
Outputs:
- coarse: bfloat16 [4, 24, 1024, 384], P(None, 'lat', 'lon')
Inputs may be any that keep to these rules, and one draw needn't show every extreme that they name: `band_ids`: band ids never fall along latitude, every band from 0 to 23 occurs, so the first and the last row lie in different bands.
All inputs are finite; a program needn't handle non-finite values.
Results may differ from a plain program's by a relative error of at most 0.015.
Values may be sent and summed in bfloat16 or wider, within the bound.
A program may use at most 128 MiB of HBM per device.

v0:
```python
import jax
import jax.numpy as jnp
from jax import lax
from jax.sharding import PartitionSpec as P

HEADS = 8
WIN_LEV = 2
WIN_LAT = 6
WIN_LON = 12


def shifted_2(block, axis, distance):
    devices = range(lax.axis_size(axis))
    route = [((i - distance) % len(devices), i) for i in devices]
    return lax.ppermute(block, axis, route)


def layer_norm(values):
    average = jnp.mean(values, axis=-1, keepdims=True)
    centred = values - average
    spread = jnp.mean(centred * centred, axis=-1, keepdims=True)
    return centred * lax.rsqrt(spread + 1e-05)


def window_attention(region, band_rows, qkv_weight, proj_weight):
    levels, lat_rows, lon_cols, model_width = region.shape
    head_count = HEADS
    head_size = model_width // head_count
    lev_win = levels // WIN_LEV
    lat_win = lat_rows // WIN_LAT
    lon_win = lon_cols // WIN_LON
    window_tokens = WIN_LEV * WIN_LAT * WIN_LON
    ordered = region.reshape(lev_win, WIN_LEV, lat_win, WIN_LAT, lon_win, WIN_LON, model_width)
    ordered = ordered.transpose(0, 2, 4, 1, 3, 5, 6).reshape(-1, model_width)
    normed = layer_norm(ordered.astype(jnp.float32)).astype(jnp.bfloat16)
    packed = jnp.dot(normed, qkv_weight, preferred_element_type=jnp.float32).astype(jnp.bfloat16)
    packed = packed.reshape(lev_win * lat_win * lon_win, window_tokens, 3, head_count, head_size)
    queries = packed[:, :, 0]
    keyset = packed[:, :, 1]
    valueset = packed[:, :, 2]
    scores = jnp.einsum(
        "wqhd,wkhd->whqk", queries, keyset, preferred_element_type=jnp.float32
    ) * head_size ** (-0.5)
    token_band = jnp.broadcast_to(
        band_rows.reshape(lat_win, 1, WIN_LAT, 1), (lat_win, WIN_LEV, WIN_LAT, WIN_LON)
    )
    token_band = token_band.reshape(lat_win, window_tokens)
    allowed = token_band[:, :, None] == token_band[:, None, :]
    allowed = jnp.broadcast_to(
        allowed[None, :, None, None], (lev_win, lat_win, lon_win, 1, window_tokens, window_tokens)
    )
    allowed = allowed.reshape(-1, 1, window_tokens, window_tokens)
    masked = jnp.where(allowed, scores, -jnp.inf)
    weights = jax.nn.softmax(masked, axis=-1).astype(jnp.bfloat16)
    attended = jnp.einsum(
        "whqk,wkhd->wqhd", weights, valueset, preferred_element_type=jnp.float32
    ).astype(jnp.bfloat16)
    attended = attended.reshape(-1, model_width)
    updated = ordered.astype(jnp.float32) + jnp.dot(
        attended, proj_weight, preferred_element_type=jnp.float32
    )
    updated = updated.astype(jnp.bfloat16).reshape(
        lev_win, lat_win, lon_win, WIN_LEV, WIN_LAT, WIN_LON, model_width
    )
    return updated.transpose(0, 3, 1, 4, 2, 5, 6).reshape(region.shape)


def feed_forward(restored, fc1_weight, fc2_weight):
    flattened = restored.reshape(-1, restored.shape[-1])
    normed = layer_norm(flattened.astype(jnp.float32)).astype(jnp.bfloat16)
    hidden = jax.nn.gelu(
        jnp.dot(normed, fc1_weight, preferred_element_type=jnp.float32), approximate=False
    ).astype(jnp.bfloat16)
    result_tokens = flattened.astype(jnp.float32) + jnp.dot(
        hidden, fc2_weight, preferred_element_type=jnp.float32
    )
    return result_tokens.astype(jnp.bfloat16).reshape(restored.shape)


def patch_merge(block_out, merge_weight):
    levels, lat_rows, lon_cols, model_width = block_out.shape
    pairs = block_out.reshape(levels, lat_rows // 2, 2, lon_cols // 2, 2 * model_width)
    upper = pairs[:, :, 0].astype(jnp.float32)
    lower = pairs[:, :, 1].astype(jnp.float32)
    total_width = 4 * model_width
    average = (
        jnp.sum(upper, axis=-1, keepdims=True) + jnp.sum(lower, axis=-1, keepdims=True)
    ) / total_width
    upper_c = upper - average
    lower_c = lower - average
    spread = (
        jnp.sum(upper_c * upper_c, axis=-1, keepdims=True)
        + jnp.sum(lower_c * lower_c, axis=-1, keepdims=True)
    ) / total_width
    scale = lax.rsqrt(spread + 1e-05)
    upper_n = (upper_c * scale).astype(jnp.bfloat16)
    lower_n = (lower_c * scale).astype(jnp.bfloat16)
    weight_upper = jnp.concatenate(
        [merge_weight[0:model_width], merge_weight[2 * model_width : 3 * model_width]], axis=0
    )
    weight_lower = jnp.concatenate(
        [
            merge_weight[model_width : 2 * model_width],
            merge_weight[3 * model_width : 4 * model_width],
        ],
        axis=0,
    )
    merged = jnp.einsum("labk,kc->lacb", upper_n, weight_upper, preferred_element_type=jnp.float32)
    merged = merged + jnp.einsum(
        "labk,kc->lacb", lower_n, weight_lower, preferred_element_type=jnp.float32
    )
    return merged.astype(jnp.bfloat16)


def body(tokens, band_ids, qkv_weight, proj_weight, fc1_weight, fc2_weight, merge_weight):
    lat_rim = WIN_LAT // 2
    lon_rim = WIN_LON // 2
    rows_dev = tokens.shape[1]
    below_rim = shifted_2(tokens[:, :lat_rim], "lat", -1)
    moved_rows = jnp.concatenate([tokens[:, lat_rim:], below_rim], axis=1)
    beside = shifted_2(moved_rows[:, :, :lon_rim], "lon", -1)
    shifted = jnp.concatenate([moved_rows[:, :, lon_rim:], beside], axis=2)
    lat_total = lax.axis_size("lat") * rows_dev
    offset = (lax.axis_index("lat") * rows_dev + lat_rim) % lat_total
    band_rows = lax.dynamic_slice_in_dim(jnp.concatenate([band_ids, band_ids]), offset, rows_dev)
    updated = window_attention(shifted, band_rows, qkv_weight, proj_weight)
    returned = shifted_2(updated[:, -lat_rim:], "lat", 1)
    restored = jnp.concatenate([returned, updated[:, :-lat_rim]], axis=1)
    returned_cols = shifted_2(restored[:, :, -lon_rim:], "lon", 1)
    restored = jnp.concatenate([returned_cols, restored[:, :, :-lon_rim]], axis=2)
    block_out = feed_forward(restored, fc1_weight, fc2_weight)
    coarse = patch_merge(block_out, merge_weight)
    relaid = lax.all_to_all(coarse, "lon", split_axis=2, concat_axis=3, tiled=True)
    return relaid


def solution(mesh):
    placed = (P(None, "lat", "lon", None), P(), P(), P(), P(), P(), P())
    return jax.shard_map(
        body, mesh=mesh, in_specs=placed, out_specs=P(None, "lat", "lon", None), check_vma=False
    )
```

profile of v0, /device:TPU:1, one launch (start us, length us, event | category | flops | bytes accessed | tf_op | source)
XLA Modules:
  0.0 225.4 jit_solution(7203858695727981345)
XLA Ops:
  0.0 2.3 %fusion.93 = (bf16[4,3,48,512]{3,2,1,0:T(8,128)(2,1)S(1)}, bf16[4,3,48,512]{3,2,1,0:T(8,128)(2,1)}) fusion(bf16[4,6,48,512]{3,2,1,0:T(8,128)(2,1)} %param.7), kind=kLoop, calls=%fused_computation.131 | loop fusion | bytes 2359296 | tf_op jit(solution)/shard_map/slice | solution.py:120
  2.3 6.9 %collective-permute-start = (bf16[4,3,48,512]{3,2,1,0:T(8,128)(2,1)}, bf16[4,3,48,512]{3,2,1,0:T(8,128)(2,1)S(1)}, u32[]{:S(2)}, u32[]{:S(2)}) collective-permute-start(bf16[4,3,48,512]{3,2,1,0:T(8,128)(2,1)} %get-tuple-element.19), channel_id=1, source_target_pairs={{16,0},{32,16},{48,32},{64,48},{80,64},{96,80},{112,96},{0,112},{1... | collective-permute-start | bytes 1769480 | tf_op jit(solution)/shard_map/ppermute | solution.py:15
  9.5 12.0 %collective-permute-done = bf16[4,3,48,512]{3,2,1,0:T(8,128)(2,1)S(1)} collective-permute-done((bf16[4,3,48,512]{3,2,1,0:T(8,128)(2,1)}, bf16[4,3,48,512]{3,2,1,0:T(8,128)(2,1)S(1)}, u32[]{:S(2)}, u32[]{:S(2)}) %collective-permute-start) | collective-permute-done | bytes 589856 | tf_op jit(solution)/shard_map/ppermute | solution.py:15
  21.5 1.6 collective-permute-start.1
  23.2 0.3 slice_maximum_fusion
  23.6 3.6 %collective-permute-done.1 = bf16[4,6,6,512]{3,2,1,0:T(8,128)(2,1)S(1)} collective-permute-done((bf16[4,6,6,512]{3,2,1,0:T(8,128)(2,1)S(1)}, bf16[4,6,6,512]{3,2,1,0:T(8,128)(2,1)S(1)}, u32[]{:S(2)}, u32[]{:S(2)}) %collective-permute-start.1) | collective-permute-done | bytes 147488 | tf_op jit(solution)/shard_map/ppermute | solution.py:15
  27.1 0.3 maximum_convert_fusion
  27.5 2.9 %copy.70 = f32[4,6,48,512]{3,0,2,1:T(4,128)} copy(f32[4,6,48,512]{3,2,1,0:T(8,128)S(1)} %maximum_convert_fusion) | data formatting | bytes 4718592 | tf_op jit(solution)/shard_map/convert_element_type | solution.py:59
  30.4 4.3 %reshape.176 = f32[2,2,1,6,4,12,512]{6,1,0,5,4,3,2:T(2,128)} reshape(f32[4,6,48,512]{3,0,2,1:T(4,128)} %copy.70) | data formatting | bytes 4718592 | tf_op jit(solution)/shard_map/convert_element_type | solution.py:59
  34.7 2.5 %bitcast_reduce_fusion = f32[2,4,2,6,12]{2,0,4,1,3:T(2,128)S(1)} fusion(f32[2,2,1,6,4,12,512]{6,1,0,5,4,3,2:T(2,128)} %reshape.176), kind=kLoop, calls=%fused_computation.95 | loop fusion | flops 588672 | bytes 2363904 | tf_op jit(solution)/shard_map/reduce_sum | solution.py:19
  37.3 0.4 copy.72
  37.7 0.4 copy.74
  38.1 3.2 %multiply_reduce_fusion.1 = f32[2,4,2,6,12]{2,0,4,1,3:T(2,128)S(1)} fusion(f32[2,4,2,6,12]{2,0,4,1,3:T(2,128)S(1)} %copy.74, f32[2,2,1,6,4,12,512]{6,1,0,5,4,3,2:T(2,128)} %reshape.176), kind=kLoop, calls=%fused_computation.38 | loop fusion | flops 1768320 | bytes 2368512 | tf_op jit(solution)/shard_map/reduce_sum | solution.py:21
  41.3 0.4 copy.75
  41.7 0.1 rsqrt.31
  41.8 4.2 %copy.71 = f32[2,1,4,2,6,12,512]{6,5,4,3,2,0,1:T(8,128)} copy(f32[2,1,4,2,6,12,512]{6,3,0,5,2,4,1:T(2,128)} %bitcast.107) | data formatting | bytes 4718592 | tf_op jit(solution)/shard_map/convert_element_type | solution.py:59
  46.0 3.9 %reshape.173 = f32[1152,512]{1,0:T(8,128)} reshape(f32[2,1,4,2,6,12,512]{6,5,4,3,2,0,1:T(8,128)} %copy.71) | data formatting | bytes 4718592 | tf_op jit(solution)/shard_map/convert_element_type | solution.py:59
  49.9 0.1 div.31
  50.0 6.0 %convolution_convert_fusion = bf16[1152,1536]{1,0:T(8,128)(2,1)} fusion(bf16[512,1536]{1,0:T(8,128)(2,1)} %param.9, f32[1152,512]{1,0:T(8,128)} %reshape.173, f32[1152]{0:T(1024)S(1)} %rsqrt.31, f32[1152]{0:T(1024)S(1)} %div.31), kind=kOutput, calls=%fused_computation.23 | convolution fusion | flops 1815478272 | bytes 7480320 | tf_op jit(solution)/shard_map/dot_general | solution.py:36
  56.0 9.6 %reshape.179 = bf16[8,144,3,8,64]{4,3,2,1,0:T(8,128)(2,1)} reshape(bf16[1152,1536]{1,0:T(8,128)(2,1)} %convolution_convert_fusion) | data formatting | bytes 7077888 | tf_op jit(solution)/shard_map/reshape | solution.py:37
  65.5 6.2 %fusion.90 = (bf16[8,144,1,8,64]{4,3,2,1,0:T(8,128)(2,1)}, bf16[8,144,1,8,64]{4,3,2,1,0:T(8,128)(2,1)}, bf16[8,144,1,8,64]{4,3,2,1,0:T(8,128)(2,1)}) fusion(bf16[8,144,3,8,64]{4,3,2,1,0:T(8,128)(2,1)} %reshape.179), kind=kLoop, calls=%fused_computation.128 | loop fusion | bytes 7077888 | tf_op jit(solution)/shard_map/slice | solution.py:40
  71.7 4.5 %copy.101 = bf16[8,144,1,8,64]{1,4,3,0,2:T(8,128)(2,1)} copy(bf16[8,144,1,8,64]{4,3,2,1,0:T(8,128)(2,1)} %get-tuple-element.10) | data formatting | bytes 2359296
  76.2 4.5 %copy.102 = bf16[8,144,1,8,64]{1,4,3,0,2:T(8,128)(2,1)} copy(bf16[8,144,1,8,64]{4,3,2,1,0:T(8,128)(2,1)} %get-tuple-element.11) | data formatting | bytes 2359296
  80.7 4.5 %copy.100 = bf16[8,144,1,8,64]{1,4,3,0,2:T(8,128)(2,1)} copy(bf16[8,144,1,8,64]{4,3,2,1,0:T(8,128)(2,1)} %get-tuple-element.9) | data formatting | bytes 2359296
  85.2 3.7 %fusion.26 = f32[8,8,144,144]{2,3,1,0:T(8,128)S(1)} fusion(bf16[8,144,1,8,64]{1,4,3,0,2:T(8,128)(2,1)} %copy.102, bf16[8,144,1,8,64]{1,4,3,0,2:T(8,128)(2,1)} %copy.101), kind=kOutput, calls=%fused_computation.47 | convolution fusion | flops 169869312 | bytes 7667712 | tf_op jit(solution)/shard_map/wqhd,wkhd->whqk/dot_general | solution.py:41
  88.9 5.2 %fusion.94 = (f32[8,8,144]{2,1,0:T(8,128)S(1)}, f32[8,8,144,144]{2,3,1,0:T(8,128)}) fusion(f32[8,8,144,144]{2,3,1,0:T(8,128)S(1)} %fusion.26, pred[144,144]{0,1:T(8,128)(4,1)S(1)} %broadcast_compare_fusion), kind=kOutput, calls=%fused_computation.132 | output fusion | flops 7962767 | bytes 10674432 | tf_op jit(solution)/shard_map/sub | solution.py:54
  94.1 4.7 %convert_bitcast_fusion = bf16[8,144,8,64]{1,3,2,0:T(8,128)(2,1)S(1)} fusion(f32[8,8,144,144]{2,3,1,0:T(8,128)} %get-tuple-element.21, f32[8,8,144]{2,1,0:T(8,128)S(1)} %get-tuple-element.20, bf16[8,144,1,8,64]{1,4,3,0,2:T(8,128)(2,1)S(1)} %copy-done.3), kind=kOutput, calls=%fused_computation.51 | convolution fusion | flops 173113344 | bytes 7704576 | tf_op jit(solution)/shard_map/whqk,wkhd->wqhd/dot_general | solution.py:55
  98.8 2.6 %copy.82 = bf16[8,144,8,64]{1,0,3,2:T(8,128)(2,1)} copy(bf16[8,144,8,64]{1,3,2,0:T(8,128)(2,1)S(1)} %convert_bitcast_fusion) | data formatting | bytes 2359296 | tf_op jit(solution)/shard_map/convert_element_type | solution.py:57
  101.4 3.7 %reshape.170 = bf16[1152,512]{0,1:T(8,128)(2,1)S(1)} reshape(bf16[8,144,8,64]{1,0,3,2:T(8,128)(2,1)} %copy.82) | data formatting | bytes 2359296 | tf_op jit(solution)/shard_map/reshape | solution.py:58
  105.1 3.7 %fusion.17 = bf16[1152,512]{1,0:T(8,128)(2,1)} fusion(f32[1152,512]{1,0:T(8,128)} %reshape.173, bf16[1152,512]{0,1:T(8,128)(2,1)S(1)} %reshape.170, bf16[512,512]{1,0:T(8,128)(2,1)} %param.10), kind=kOutput, calls=%fused_computation.32 | convolution fusion | flops 605159424 | bytes 5242880 | tf_op jit(solution)/shard_map/dot_general | solution.py:59
  108.7 3.2 %reshape.171 = bf16[2,1,4,2,6,12,512]{6,5,4,3,2,0,1:T(8,128)(2,1)} reshape(bf16[1152,512]{1,0:T(8,128)(2,1)} %fusion.17) | data formatting | bytes 2359296 | tf_op jit(solution)/shard_map/reshape | solution.py:62
  111.9 2.6 %copy.83 = bf16[2,2,1,6,4,12,512]{6,1,0,5,4,3,2:T(2,128)(2,1)S(1)} copy(bf16[2,2,1,6,4,12,512]{6,5,3,1,4,0,2:T(8,128)(2,1)} %bitcast.111) | data formatting | bytes 2359296 | tf_op jit(solution)/shard_map/transpose | solution.py:65
  114.5 1.3 reshape.172
  115.8 1.6 fusion.92
  117.5 2.7 %collective-permute-start.2 = (bf16[4,3,48,512]{3,0,2,1:T(4,128)(2,1)S(1)}, bf16[4,3,48,512]{3,0,2,1:T(4,128)(2,1)S(1)}, u32[]{:S(2)}, u32[]{:S(2)}) collective-permute-start(bf16[4,3,48,512]{3,0,2,1:T(4,128)(2,1)S(1)} %get-tuple-element.16), channel_id=1, source_target_pairs={{112,0},{0,16},{16,32},{32,48},{48,64},{64,80},{80,96},{96,112},{1... | collective-permute-start | bytes 1769480 | tf_op jit(solution)/shard_map/ppermute | solution.py:15
  120.2 16.4 %collective-permute-done.2 = bf16[4,3,48,512]{3,0,2,1:T(4,128)(2,1)S(1)} collective-permute-done((bf16[4,3,48,512]{3,0,2,1:T(4,128)(2,1)S(1)}, bf16[4,3,48,512]{3,0,2,1:T(4,128)(2,1)S(1)}, u32[]{:S(2)}, u32[]{:S(2)}) %collective-permute-start.2) | collective-permute-done | bytes 589856 | tf_op jit(solution)/shard_map/ppermute | solution.py:15
  136.6 0.1 pad_maximum_fusion.2
  136.7 4.2 %fusion.91 = (bf16[512,1024]{1,0:T(8,128)(2,1)}, bf16[512,1024]{1,0:T(8,128)(2,1)}, bf16[512,1024]{1,0:T(8,128)(2,1)}, bf16[512,1024]{1,0:T(8,128)(2,1)}) fusion(bf16[2048,1024]{1,0:T(8,128)(2,1)} %param.13), kind=kLoop, calls=%fused_computation.129 | loop fusion | bytes 8388608 | tf_op jit(solution)/shard_map/slice | solution.py:103
  141.0 0.7 fusion.89
  141.7 0.7 broadcast_multiply_fusion
  142.3 1.0 copy.86
  143.3 2.9 %multiply_reduce_fusion = f32[4,6,48]{0,2,1:T(8,128)S(1)} fusion(f32[4,6,48]{0,2,1:T(8,128)} %broadcast_multiply_fusion, bf16[4,3,48,512]{3,0,2,1:T(4,128)(2,1)S(1)} %get-tuple-element.17, bf16[4,3,48,512]{3,0,2,1:T(4,128)(2,1)S(1)} %collective-permute-done.2, bf16[4,6,6,512]{3,0,2,1:T(4,128)(2,1)S(1)} %collective-permute-done.3), kind=kLoop, calls=%fused_computation.36 | loop fusion | flops 3537792 | bytes 1336320 | tf_op jit(solution)/shard_map/reduce_sum | solution.py:21
  146.3 0.7 add_rsqrt_fusion
  147.0 1.0 copy.89
  148.0 0.1 rsqrt.33
  148.1 0.8 fusion.46
  148.9 0.8 copy.84
  149.7 1.4 copy-done.2
  151.1 0.4 fusion.19
  151.5 26.3 %fusion.16 = bf16[1152,512]{1,0:T(8,128)(2,1)} fusion(f32[1152,512]{1,0:T(8,128)} %bitcast.110, bf16[2048,512]{1,0:T(8,128)(2,1)S(1)} %copy-done, bf16[1152,512]{1,0:T(8,128)(2,1)S(1)} %fusion.19, bf16[512,2048]{1,0:T(8,128)(2,1)} %param.11), kind=kOutput, calls=%fused_computation.31 | convolution fusion | flops 4986372096 | bytes 8912896 | tf_op jit(solution)/shard_map/dot_general | solution.py:74
  177.8 2.5 %reshape_reshape.3 = bf16[4,3,2,24,1024]{4,3,2,1,0:T(8,128)(2,1)S(1)} reshape(bf16[1152,512]{1,0:T(8,128)(2,1)} %fusion.16) | data formatting | bytes 2359296 | tf_op jit(solution)/shard_map/reshape;reshape | solution.py:82
  180.2 0.2 convert_reduce_fusion
  180.5 0.4 fusion.43
  180.9 0.5 copy-done.7
  181.4 0.8 fusion.20
  182.3 0.4 copy-done.4
  182.7 0.3 copy-done.5
  183.0 0.8 fusion.34
  183.8 3.7 %copy.92 = bf16[4,3,1024,24]{3,0,1,2:T(4,128)(2,1)} copy(bf16[4,3,1024,24]{2,3,1,0:T(8,128)(2,1)S(1)} %fusion.34) | data formatting | bytes 1179648 | tf_op jit(solution)/shard_map/convert_element_type | solution.py:112
  187.5 8.5 %reshape.180 = bf16[16,2,9216]{2,1,0:T(2,128)(2,1)S(1)} reshape(bf16[1024,3,4,24]{3,2,1,0:T(4,128)(2,1)} %bitcast.108) | data formatting | bytes 1179648
  196.0 17.8 %all_to_all.18 = bf16[16,2,9216]{2,1,0:T(2,128)(2,1)S(1)} all-to-all(bf16[16,2,9216]{2,1,0:T(2,128)(2,1)S(1)} %reshape.180), channel_id=1, replica_groups=mesh['lat'=8,'lon'=16] {'lon'}, dimensions={0} | all-to-all | bytes 1179648 | tf_op jit(solution)/shard_map/all_to_all | solution.py:133
  213.8 5.7 %reshape.181 = bf16[1024,3,4,24]{3,2,1,0:T(4,128)(2,1)} reshape(bf16[16,2,9216]{2,1,0:T(2,128)(2,1)S(1)} %all_to_all.18) | data formatting | bytes 1179648
  219.5 4.5 %copy.93 = bf16[4,3,16,64,24]{3,4,2,1,0:T(8,128)(2,1)S(1)} copy(bf16[4,3,16,64,24]{4,0,1,3,2:T(4,128)(2,1)} %bitcast.109) | data formatting | bytes 1179648 | tf_op jit(solution)/shard_map/all_to_all | solution.py:133
  224.0 1.3 copy.94
  (29 shorter events, 0.7 us)
Async XLA Ops:
  0.0 151.5 %copy-start = (bf16[2048,512]{1,0:T(8,128)(2,1)S(1)}, bf16[2048,512]{1,0:T(8,128)(2,1)}, u32[]{:S(2)}) copy-start(bf16[2048,512]{1,0:T(8,128)(2,1)} %param.12) | copy-start | bytes 6291460
  0.0 9.2 %copy-start.8 = (s32[48]{0:T(128)S(1)}, s32[48]{0:T(128)}, u32[]{:S(2)}) copy-start(s32[48]{0:T(128)} %param.8) | copy-start | bytes 580
  2.3 19.2 %collective-permute-start = (bf16[4,3,48,512]{3,2,1,0:T(8,128)(2,1)}, bf16[4,3,48,512]{3,2,1,0:T(8,128)(2,1)S(1)}, u32[]{:S(2)}, u32[]{:S(2)}) collective-permute-start(bf16[4,3,48,512]{3,2,1,0:T(8,128)(2,1)} %get-tuple-element.19), channel_id=1, source_target_pairs={{16,0},{32,16},{48,32},{64,48},{80,64},{96,80},{112,96},{0,112},{1... | collective-permute-start | bytes 1769480 | tf_op jit(solution)/shard_map/ppermute | solution.py:15
  21.5 5.6 %collective-permute-start.1 = (bf16[4,6,6,512]{3,2,1,0:T(8,128)(2,1)S(1)}, bf16[4,6,6,512]{3,2,1,0:T(8,128)(2,1)S(1)}, u32[]{:S(2)}, u32[]{:S(2)}) collective-permute-start(bf16[4,6,6,512]{3,2,1,0:T(8,128)(2,1)S(1)} %pad_maximum_fusion.1), channel_id=1, source_target_pairs={{1,0},{2,1},{3,2},{4,3},{5,4},{6,5},{7,6},{8,7},{9,8},{10,9},{11,1... | collective-permute-start | bytes 442376 | tf_op jit(solution)/shard_map/ppermute | solution.py:15
  88.9 5.2 %copy-start.3 = (bf16[8,144,1,8,64]{1,4,3,0,2:T(8,128)(2,1)S(1)}, bf16[8,144,1,8,64]{1,4,3,0,2:T(8,128)(2,1)}, u32[]{:S(2)}) copy-start(bf16[8,144,1,8,64]{1,4,3,0,2:T(8,128)(2,1)} %copy.100) | copy-start | bytes 3538948
  117.5 19.1 %collective-permute-start.2 = (bf16[4,3,48,512]{3,0,2,1:T(4,128)(2,1)S(1)}, bf16[4,3,48,512]{3,0,2,1:T(4,128)(2,1)S(1)}, u32[]{:S(2)}, u32[]{:S(2)}) collective-permute-start(bf16[4,3,48,512]{3,0,2,1:T(4,128)(2,1)S(1)} %get-tuple-element.16), channel_id=1, source_target_pairs={{112,0},{0,16},{16,32},{32,48},{48,64},{64,80},{80,96},{96,112},{1... | collective-permute-start | bytes 1769480 | tf_op jit(solution)/shard_map/ppermute | solution.py:15
  136.7 4.3 %collective-permute-start.3 = (bf16[4,6,6,512]{3,0,2,1:T(4,128)(2,1)S(1)}, bf16[4,6,6,512]{3,0,2,1:T(4,128)(2,1)S(1)}, u32[]{:S(2)}, u32[]{:S(2)}) collective-permute-start(bf16[4,6,6,512]{3,0,2,1:T(4,128)(2,1)S(1)} %pad_maximum_fusion.2), channel_id=1, source_target_pairs={{15,0},{0,1},{1,2},{2,3},{3,4},{4,5},{5,6},{6,7},{7,8},{8,9},{9,10... | collective-permute-start | bytes 442376 | tf_op jit(solution)/shard_map/ppermute | solution.py:15
  149.7 1.4 copy-start.2
  177.8 3.2 %copy-start.6 = (bf16[512,1024]{1,0:T(8,128)(2,1)S(1)}, bf16[512,1024]{1,0:T(8,128)(2,1)}, u32[]{:S(2)}) copy-start(bf16[512,1024]{1,0:T(8,128)(2,1)} %get-tuple-element.13) | copy-start | bytes 3145732
  180.2 1.2 copy-start.7
  181.4 1.2 copy-start.4
  181.4 1.5 copy-start.5
  219.5 5.8 %copy-start.1 = (bf16[2048,512]{1,0:T(8,128)(2,1)S(1)}, bf16[2048,512]{1,0:T(8,128)(2,1)}, u32[]{:S(2)}) copy-start(bf16[2048,512]{1,0:T(8,128)(2,1)} %param.12) | copy-start | bytes 6291460
where the time goes:
time: 230 us; the launch traced here: 225 us
  local copies, waits for them, and re-layouts  99.4 us (43%)
  matrix products  45.9 us (20%)
  waiting for transfers between devices  31.9 us (14%)
  other arithmetic  18.6 us (8%)
  blocking collectives  17.8 us (8%)
  starting transfers between devices  11.3 us (5%)
    ppermute x4, waiting for transfers between devices, shifted_2(): return lax.ppermute(block, axis, route)  31.9 us
    unnamed x23, local copies, waits for them, and re-layouts  30.3 us
    dot_general x1, matrix products, feed_forward(): jnp.dot(hidden, fc2_weight, preferred_element_type=jnp.float32)  26.3 us
    all_to_all x1, blocking collectives, body(): lax.all_to_all(coarse, 'lon', split_axis=2, concat_axis=3, tiled=True)  17.8 us
    convert_element_type x4, local copies, waits for them, and re-layouts, window_attention(): ordered.astype(jnp.float32)  15.3 us
    ppermute x4, starting transfers between devices, shifted_2(): return lax.ppermute(block, axis, route)  11.3 us
    reshape x1, local copies, waits for them, and re-layouts, window_attention(): packed.reshape(lev_win * lat_win * lon_win, window_tokens, 3, head_count,...  9.55 us
    slice x1, local copies, waits for them, and re-layouts, window_attention(): valueset = packed[:, :, 2]  6.21 us
  transfers between devices with their start and end apart: 4, of which 3 were waited for; matrix products, arithmetic and copies ran while one was open for 2% of the time, Pallas kernels for 0%

commit v1 on v0

--- a/solution.py
+++ b/solution.py
@@ -1,12 +1,20 @@
+import functools
+
 import jax
 import jax.numpy as jnp
 from jax import lax
+from jax.experimental import pallas as pl
+from jax.experimental.pallas import tpu as pltpu
 from jax.sharding import PartitionSpec as P
 
 HEADS = 8
 WIN_LEV = 2
 WIN_LAT = 6
 WIN_LON = 12
+MESH = pl.DeviceIdType.MESH
+BF16 = jnp.bfloat16
+F32 = jnp.float32
+PEERS = 16
 
 
 def shifted_2(block, axis, distance):
@@ -65,51 +73,124 @@
     return updated.transpose(0, 3, 1, 4, 2, 5, 6).reshape(region.shape)
 
 
-def feed_forward(restored, fc1_weight, fc2_weight):
-    flattened = restored.reshape(-1, restored.shape[-1])
-    normed = layer_norm(flattened.astype(jnp.float32)).astype(jnp.bfloat16)
-    hidden = jax.nn.gelu(
-        jnp.dot(normed, fc1_weight, preferred_element_type=jnp.float32), approximate=False
-    ).astype(jnp.bfloat16)
-    result_tokens = flattened.astype(jnp.float32) + jnp.dot(
-        hidden, fc2_weight, preferred_element_type=jnp.float32
-    )
-    return result_tokens.astype(jnp.bfloat16).reshape(restored.shape)
-
-
-def patch_merge(block_out, merge_weight):
-    levels, lat_rows, lon_cols, model_width = block_out.shape
-    pairs = block_out.reshape(levels, lat_rows // 2, 2, lon_cols // 2, 2 * model_width)
-    upper = pairs[:, :, 0].astype(jnp.float32)
-    lower = pairs[:, :, 1].astype(jnp.float32)
-    total_width = 4 * model_width
-    average = (
-        jnp.sum(upper, axis=-1, keepdims=True) + jnp.sum(lower, axis=-1, keepdims=True)
-    ) / total_width
-    upper_c = upper - average
-    lower_c = lower - average
-    spread = (
-        jnp.sum(upper_c * upper_c, axis=-1, keepdims=True)
-        + jnp.sum(lower_c * lower_c, axis=-1, keepdims=True)
-    ) / total_width
+def dot(a, b):
+    return jnp.dot(a, b, preferred_element_type=F32)
+
+
+def finish_group(restored, fc1, fc2, merge, acc, block):
+    normed = layer_norm(restored[...].astype(F32)).astype(BF16)
+    part = 512
+
+    def step(i, carry):
+        cols = pl.ds(pl.multiple_of(i * part, part), part)
+        pre = dot(normed, fc1[:, cols])
+        hidden = (0.5 * pre * (1.0 + lax.erf(pre * 0.7071067811865476))).astype(BF16)
+        acc[...] += dot(hidden, fc2[cols, :])
+        return carry
+
+    acc[...] = restored[...].astype(F32)
+    lax.fori_loop(0, 4, step, 0)
+    pieces = [acc[pl.ds(144 * i, 144), :].astype(BF16).astype(F32) for i in range(4)]
+    average = sum(jnp.sum(p, axis=-1, keepdims=True) for p in pieces) / 2048
+    pieces = [p - average for p in pieces]
+    spread = sum(jnp.sum(p * p, axis=-1, keepdims=True) for p in pieces) / 2048
     scale = lax.rsqrt(spread + 1e-05)
-    upper_n = (upper_c * scale).astype(jnp.bfloat16)
-    lower_n = (lower_c * scale).astype(jnp.bfloat16)
-    weight_upper = jnp.concatenate(
-        [merge_weight[0:model_width], merge_weight[2 * model_width : 3 * model_width]], axis=0
-    )
-    weight_lower = jnp.concatenate(
-        [
-            merge_weight[model_width : 2 * model_width],
-            merge_weight[3 * model_width : 4 * model_width],
+    merged = None
+    for i, p in enumerate(pieces):
+        term = dot((p * scale).astype(BF16), merge[pl.ds(512 * i, 512), :])
+        merged = term if merged is None else merged + term
+    return merged
+
+
+def pack_group(merged, send):
+    low = lax.broadcasted_iota(jnp.int32, (72, 128), 1) < 64
+    pad = jnp.zeros((8, 128), F32)
+    for j in range(8):
+        one = merged[0:72, 128 * j : 128 * j + 128]
+        two = merged[72:144, 128 * j : 128 * j + 128]
+        even = jnp.where(low, one, pltpu.roll(two, 64, 1))
+        odd = jnp.where(low, pltpu.roll(one, 64, 1), two)
+        send[2 * j] = jnp.concatenate([even, pad], axis=0).astype(BF16)
+        send[2 * j + 1] = jnp.concatenate([odd, pad], axis=0).astype(BF16)
+
+
+def unpack_group(got, out, group):
+    for a in range(3):
+        lines = jnp.concatenate(
+            [got[s].astype(F32)[24 * a : 24 * a + 24, :] for s in range(PEERS)], axis=0
+        )
+        turned = lines.T
+        out[2 * group, a] = turned[0:64, :].astype(BF16)
+        out[2 * group + 1, a] = turned[64:128, :].astype(BF16)
+
+
+def finish_kernel(
+    restored, fc1_hbm, fc2_hbm, merge_hbm, out,
+    fc1, fc2, merge, acc, send, got, weight_sem, send_sem, recv_sem, own_sem,
+):
+    loads = [
+        pltpu.make_async_copy(src, dst, weight_sem.at[i])
+        for i, (src, dst) in enumerate([(fc1_hbm, fc1), (fc2_hbm, fc2), (merge_hbm, merge)])
+    ]
+    for c in loads:
+        c.start()
+    me = lax.axis_index("lon")
+    barrier = pltpu.get_barrier_semaphore()
+    for d in range(1, PEERS):
+        pl.semaphore_signal(
+            barrier, inc=1, device_id={"lon": lax.rem(me + d, PEERS)}, device_id_type=MESH
+        )
+    pl.semaphore_wait(barrier, PEERS - 1)
+    for c in loads:
+        c.wait()
+    copies = [[], []]
+    for g in range(2):
+        merged = finish_group(restored.at[g], fc1, fc2, merge, acc, None)
+        pack_group(merged, send.at[g])
+        for d in range(1, PEERS):
+            to = lax.rem(me + d, PEERS)
+            c = pltpu.make_async_remote_copy(
+                src_ref=send.at[g, to], dst_ref=got.at[g, me],
+                send_sem=send_sem.at[g, d], recv_sem=recv_sem.at[g, d],
+                device_id={"lon": to}, device_id_type=MESH,
+            )
+            c.start()
+            copies[g].append(c)
+        own = pltpu.make_async_copy(send.at[g, me], got.at[g, me], own_sem.at[g])
+        own.start()
+        copies[g].append(own)
+    for g in range(2):
+        for c in copies[g]:
+            c.wait()
+        unpack_group(got.at[g], out, g)
+
+
+def finish(restored, fc1_weight, fc2_weight, merge_weight):
+    hbm = pl.BlockSpec(memory_space=pl.ANY)
+    vmem = pl.BlockSpec(memory_space=pltpu.VMEM)
+    dma = pltpu.SemaphoreType.DMA
+    return pl.pallas_call(
+        finish_kernel,
+        out_shape=jax.ShapeDtypeStruct((4, 3, 64, 384), BF16),
+        in_specs=[vmem, hbm, hbm, hbm],
+        out_specs=vmem,
+        scratch_shapes=[
+            pltpu.VMEM((512, 2048), BF16),
+            pltpu.VMEM((2048, 512), BF16),
+            pltpu.VMEM((2048, 1024), BF16),
+            pltpu.VMEM((576, 512), F32),
+            pltpu.VMEM((2, PEERS, 80, 128), BF16),
+            pltpu.VMEM((2, PEERS, 80, 128), BF16),
+            dma((3,)),
+            dma((2, PEERS)),
+            dma((2, PEERS)),
+            dma((2,)),
         ],
-        axis=0,
-    )
-    merged = jnp.einsum("labk,kc->lacb", upper_n, weight_upper, preferred_element_type=jnp.float32)
-    merged = merged + jnp.einsum(
-        "labk,kc->lacb", lower_n, weight_lower, preferred_element_type=jnp.float32
-    )
-    return merged.astype(jnp.bfloat16)
+        compiler_params=pltpu.CompilerParams(
+            collective_id=0, has_side_effects=True, vmem_limit_bytes=56 * 1024 * 1024
+        ),
+        name="finish",
+    )(restored, fc1_weight, fc2_weight, merge_weight)
 
 
 def body(tokens, band_ids, qkv_weight, proj_weight, fc1_weight, fc2_weight, merge_weight):
@@ -128,10 +209,8 @@
     restored = jnp.concatenate([returned, updated[:, :-lat_rim]], axis=1)
     returned_cols = shifted_2(restored[:, :, -lon_rim:], "lon", 1)
     restored = jnp.concatenate([returned_cols, restored[:, :, :-lon_rim]], axis=2)
-    block_out = feed_forward(restored, fc1_weight, fc2_weight)
-    coarse = patch_merge(block_out, merge_weight)
-    relaid = lax.all_to_all(coarse, "lon", split_axis=2, concat_axis=3, tiled=True)
-    return relaid
+    ordered = restored.reshape(2, 2, 3, 2, 24, 2, 512).transpose(0, 5, 3, 1, 2, 4, 6)
+    return finish(ordered.reshape(2, 576, 512), fc1_weight, fc2_weight, merge_weight)
 
 
 def solution(mesh):

time: 230 us -> 166 us (0.72); the launches traced: 225 us -> 165 us
  local copies, waits for them, and re-layouts: 99.4 us -> 63.9 us
  matrix products: 45.9 us -> 16.3 us
  Pallas kernels: 0 us -> 26.6 us
  blocking collectives: 17.8 us -> 0 us
  other arithmetic: 18.6 us -> 12.5 us
    dot_general x3 -> x0, matrix products: 27.9 us -> none  [the longest x1 26.3 us: feed_forward(): jnp.dot(hidden, fc2_weight, preferred_element_type=jnp.float32)]
    pallas_call x0 -> x1, Pallas kernels: none -> 26.6 us  [finish(): pl.pallas_call(finish_kernel, out_shape=jax.ShapeDtypeStruct((4, 3, 64, 3...]
    all_to_all x1 -> x0, blocking collectives: 17.8 us -> none  [body(): lax.all_to_all(coarse, 'lon', split_axis=2, concat_axis=3, tiled=True)]
    unnamed x23 -> x14, local copies, waits for them, and re-layouts: 30.3 us -> 15.5 us
    all_to_all x2 -> x0, local copies, waits for them, and re-layouts: 5.77 us -> none  [body(): lax.all_to_all(coarse, 'lon', split_axis=2, concat_axis=3, tiled=True)]
    convert_element_type x2 -> x0, local copies, waits for them, and re-layouts: 4.42 us -> none  [the longest x1 3.66 us: patch_merge(): return merged.astype(jnp.bfloat16)]
    slice x1 -> x0, local copies, waits for them, and re-layouts: 4.24 us -> none  [patch_merge(): merge_weight[model_width:2 * model_width]]
    reduce_sum x2 -> x1, other arithmetic: 6.09 us -> 3.16 us  [layer_norm(): spread = jnp.mean(centred * centred, axis=-1, keepdims=True)]
  transfers between devices with their start and end apart: 4 -> 4, of which waited for: 3 -> 4; matrix products, arithmetic and copies ran while one was open for 2% -> 0% of each run, Pallas kernels for 0% -> 0%
where the time goes in v1:
time: 166 us; the launch traced here: 165 us
  local copies, waits for them, and re-layouts  63.9 us (38%)
  waiting for transfers between devices  34 us (20%)
  Pallas kernels  26.6 us (16%)
  matrix products  16.3 us (10%)
  other arithmetic  12.5 us (8%)
  starting transfers between devices  11.5 us (7%)
    ppermute x4, waiting for transfers between devices, shifted_2(): return lax.ppermute(block, axis, route)  34 us
    pallas_call x1, Pallas kernels, finish(): pl.pallas_call(finish_kernel, out_shape=jax.ShapeDtypeStruct((4, 3, 64, 3...  26.6 us
    unnamed x14, local copies, waits for them, and re-layouts  15.5 us
    convert_element_type x4, local copies, waits for them, and re-layouts, window_attention(): ordered.astype(jnp.float32)  15.2 us
    ppermute x4, starting transfers between devices, shifted_2(): return lax.ppermute(block, axis, route)  11.5 us
    reshape x1, local copies, waits for them, and re-layouts, window_attention(): packed.reshape(lev_win * lat_win * lon_win, window_tokens, 3, head_count,...  9.52 us
    slice x1, local copies, waits for them, and re-layouts, window_attention(): valueset = packed[:, :, 2]  6.13 us
    dot_general x1, matrix products, window_attention(): jnp.dot(normed, qkv_weight, preferred_element_type=jnp.float32)  5.52 us
  transfers between devices with their start and end apart: 4, of which 4 were waited for; matrix products, arithmetic and copies ran while one was open for 0% of the time, Pallas kernels for 0%

profile of v1, /device:TPU:1, one launch (start us, length us, event | category | flops | bytes accessed | tf_op | source)
XLA Modules:
  0.0 165.1 jit_solution(17188551451772571758)
XLA Ops:
  0.0 0.0 copy-start
  0.0 0.0 copy-start.4
  0.0 1.5 fusion.20
  1.5 6.9 %collective-permute-start = (bf16[4,3,48,512]{3,2,1,0:T(8,128)(2,1)S(1)}, bf16[4,3,48,512]{3,2,1,0:T(8,128)(2,1)S(1)}, u32[]{:S(2)}, u32[]{:S(2)}) collective-permute-start(bf16[4,3,48,512]{3,2,1,0:T(8,128)(2,1)S(1)} %get-tuple-element.11), channel_id=1, source_target_pairs={{16,0},{32,16},{48,32},{64,48},{80,64},{96,80},{112,96},{0,112},{1... | collective-permute-start | bytes 1769480 | tf_op jit(solution)/shard_map/ppermute | solution.py:23
  8.4 0.0 copy-done.4
  8.4 0.1 pad_add_fusion
  8.5 0.1 dynamic_slice.3
  8.6 0.1 broadcast_in_dim.10
  8.7 0.1 eq.23
  8.7 11.7 %collective-permute-done = bf16[4,3,48,512]{3,2,1,0:T(8,128)(2,1)S(1)} collective-permute-done((bf16[4,3,48,512]{3,2,1,0:T(8,128)(2,1)S(1)}, bf16[4,3,48,512]{3,2,1,0:T(8,128)(2,1)S(1)}, u32[]{:S(2)}, u32[]{:S(2)}) %collective-permute-start) | collective-permute-done | bytes 589856 | tf_op jit(solution)/shard_map/ppermute | solution.py:23
  20.4 1.6 collective-permute-start.1
  22.1 0.1 broadcast_compare_fusion
  22.2 0.3 slice_maximum_fusion
  22.5 3.6 %collective-permute-done.1 = bf16[4,6,6,512]{3,2,1,0:T(8,128)(2,1)S(1)} collective-permute-done((bf16[4,6,6,512]{3,2,1,0:T(8,128)(2,1)S(1)}, bf16[4,6,6,512]{3,2,1,0:T(8,128)(2,1)S(1)}, u32[]{:S(2)}, u32[]{:S(2)}) %collective-permute-start.1) | collective-permute-done | bytes 147488 | tf_op jit(solution)/shard_map/ppermute | solution.py:23
  26.0 0.3 maximum_convert_fusion
  26.4 2.9 %copy.38 = f32[4,6,48,512]{3,0,2,1:T(4,128)} copy(f32[4,6,48,512]{3,2,1,0:T(8,128)S(1)} %maximum_convert_fusion) | data formatting | bytes 4718592 | tf_op jit(solution)/shard_map/convert_element_type | solution.py:67
  29.3 4.2 %reshape.126 = f32[2,2,1,6,4,12,512]{6,1,0,5,4,3,2:T(2,128)} reshape(f32[4,6,48,512]{3,0,2,1:T(4,128)} %copy.38) | data formatting | bytes 4718592 | tf_op jit(solution)/shard_map/convert_element_type | solution.py:67
  33.5 2.5 %bitcast_reduce_fusion = f32[2,4,2,6,12]{2,0,4,1,3:T(2,128)S(1)} fusion(f32[2,2,1,6,4,12,512]{6,1,0,5,4,3,2:T(2,128)} %reshape.126), kind=kLoop, calls=%fused_computation.32 | loop fusion | flops 588672 | bytes 2363904 | tf_op jit(solution)/shard_map/reduce_sum | solution.py:27
  36.0 0.4 copy.40
  36.5 0.4 copy.42
  36.9 0.1 div.17
  37.0 3.2 %multiply_reduce_fusion = f32[2,4,2,6,12]{2,0,4,1,3:T(2,128)S(1)} fusion(f32[2,4,2,6,12]{2,0,4,1,3:T(2,128)S(1)} %copy.42, f32[2,2,1,6,4,12,512]{6,1,0,5,4,3,2:T(2,128)} %reshape.126), kind=kLoop, calls=%fused_computation.13 | loop fusion | flops 1768320 | bytes 2368512 | tf_op jit(solution)/shard_map/reduce_sum | solution.py:29
  40.1 0.4 copy.43
  40.6 0.1 rsqrt.12
  40.7 4.1 %copy.39 = f32[2,1,4,2,6,12,512]{6,5,4,3,2,0,1:T(8,128)} copy(f32[2,1,4,2,6,12,512]{6,3,0,5,2,4,1:T(2,128)} %bitcast.35) | data formatting | bytes 4718592 | tf_op jit(solution)/shard_map/convert_element_type | solution.py:67
  44.8 3.9 %reshape.124 = f32[1152,512]{1,0:T(8,128)} reshape(f32[2,1,4,2,6,12,512]{6,5,4,3,2,0,1:T(8,128)} %copy.39) | data formatting | bytes 4718592 | tf_op jit(solution)/shard_map/convert_element_type | solution.py:67
  48.8 0.0 copy-done
  48.8 5.5 %convolution_convert_fusion = bf16[1152,1536]{1,0:T(8,128)(2,1)} fusion(bf16[512,1536]{1,0:T(8,128)(2,1)S(1)} %copy-done, f32[1152,512]{1,0:T(8,128)} %reshape.124, f32[1152]{0:T(1024)S(1)} %rsqrt.12, f32[1152]{0:T(1024)S(1)} %div.17), kind=kOutput, calls=%fused_computation.4 | convolution fusion | flops 1815478272 | bytes 7480320 | tf_op jit(solution)/shard_map/dot_general | solution.py:44
  54.3 9.5 %reshape.128 = bf16[8,144,3,8,64]{4,3,2,1,0:T(8,128)(2,1)} reshape(bf16[1152,1536]{1,0:T(8,128)(2,1)} %convolution_convert_fusion) | data formatting | bytes 7077888 | tf_op jit(solution)/shard_map/reshape | solution.py:45
  63.8 6.1 %fusion.18 = (bf16[8,144,1,8,64]{4,3,2,1,0:T(8,128)(2,1)}, bf16[8,144,1,8,64]{4,3,2,1,0:T(8,128)(2,1)}, bf16[8,144,1,8,64]{4,3,2,1,0:T(8,128)(2,1)}) fusion(bf16[8,144,3,8,64]{4,3,2,1,0:T(8,128)(2,1)} %reshape.128), kind=kLoop, calls=%fused_computation.34 | loop fusion | bytes 7077888 | tf_op jit(solution)/shard_map/slice | solution.py:48
  69.9 4.5 %copy.59 = bf16[8,144,1,8,64]{1,4,3,0,2:T(8,128)(2,1)} copy(bf16[8,144,1,8,64]{4,3,2,1,0:T(8,128)(2,1)} %get-tuple-element.5) | data formatting | bytes 2359296
  74.4 4.5 %copy.60 = bf16[8,144,1,8,64]{1,4,3,0,2:T(8,128)(2,1)} copy(bf16[8,144,1,8,64]{4,3,2,1,0:T(8,128)(2,1)} %get-tuple-element.6) | data formatting | bytes 2359296
  78.9 4.5 %copy.61 = bf16[8,144,1,8,64]{1,4,3,0,2:T(8,128)(2,1)} copy(bf16[8,144,1,8,64]{4,3,2,1,0:T(8,128)(2,1)} %get-tuple-element.7) | data formatting | bytes 2359296
  83.4 3.7 %fusion.7 = f32[8,8,144,144]{2,3,1,0:T(8,128)S(1)} fusion(bf16[8,144,1,8,64]{1,4,3,0,2:T(8,128)(2,1)} %copy.61, bf16[8,144,1,8,64]{1,4,3,0,2:T(8,128)(2,1)} %copy.60), kind=kOutput, calls=%fused_computation.14 | convolution fusion | flops 169869312 | bytes 7667712 | tf_op jit(solution)/shard_map/wqhd,wkhd->whqk/dot_general | solution.py:49
  87.1 0.0 copy-start.2
  87.1 5.0 %fusion.21 = (f32[8,8,144]{2,1,0:T(8,128)S(1)}, f32[8,8,144,144]{2,3,1,0:T(8,128)}) fusion(f32[8,8,144,144]{2,3,1,0:T(8,128)S(1)} %fusion.7, pred[144,144]{0,1:T(8,128)(4,1)S(1)} %broadcast_compare_fusion), kind=kOutput, calls=%fused_computation.37 | output fusion | flops 7962767 | bytes 10674432 | tf_op jit(solution)/shard_map/sub | solution.py:62
  92.1 0.0 copy-done.2
  92.1 4.6 %convert_bitcast_fusion = bf16[8,144,8,64]{1,3,2,0:T(8,128)(2,1)S(1)} fusion(f32[8,8,144,144]{2,3,1,0:T(8,128)} %get-tuple-element.13, f32[8,8,144]{2,1,0:T(8,128)S(1)} %get-tuple-element.12, bf16[8,144,1,8,64]{1,4,3,0,2:T(8,128)(2,1)S(1)} %copy-done.2), kind=kOutput, calls=%fused_computation.18 | convolution fusion | flops 173113344 | bytes 7704576 | tf_op jit(solution)/shard_map/whqk,wkhd->wqhd/dot_general | solution.py:63
  96.8 2.6 %copy.50 = bf16[8,144,8,64]{1,0,3,2:T(8,128)(2,1)} copy(bf16[8,144,8,64]{1,3,2,0:T(8,128)(2,1)S(1)} %convert_bitcast_fusion) | data formatting | bytes 2359296 | tf_op jit(solution)/shard_map/convert_element_type | solution.py:65
  99.4 0.0 copy-start.3
  99.4 3.7 %reshape.119 = bf16[1152,512]{0,1:T(8,128)(2,1)S(1)} reshape(bf16[8,144,8,64]{1,0,3,2:T(8,128)(2,1)} %copy.50) | data formatting | bytes 2359296 | tf_op jit(solution)/shard_map/reshape | solution.py:66
  103.1 0.0 copy-done.3
  103.1 2.5 %fusion.6 = bf16[1152,512]{1,0:T(8,128)(2,1)S(1)} fusion(f32[1152,512]{1,0:T(8,128)} %reshape.124, bf16[1152,512]{0,1:T(8,128)(2,1)S(1)} %reshape.119, bf16[512,512]{1,0:T(8,128)(2,1)S(1)} %copy-done.3), kind=kOutput, calls=%fused_computation.11 | convolution fusion | flops 605159424 | bytes 5242880 | tf_op jit(solution)/shard_map/dot_general | solution.py:67
  105.6 0.3 reshape.120
  105.9 2.2 %copy.51 = bf16[2,2,1,6,4,12,512]{6,1,0,5,4,3,2:T(2,128)(2,1)} copy(bf16[2,2,1,6,4,12,512]{6,5,3,1,4,0,2:T(8,128)(2,1)S(1)} %bitcast.36) | data formatting | bytes 2359296 | tf_op jit(solution)/shard_map/transpose | solution.py:73
  108.1 3.2 %reshape.121 = bf16[4,6,48,512]{3,0,2,1:T(4,128)(2,1)S(1)} reshape(bf16[2,2,1,6,4,12,512]{6,1,0,5,4,3,2:T(2,128)(2,1)} %copy.51) | data formatting | bytes 2359296 | tf_op jit(solution)/shard_map/reshape | solution.py:73
  111.3 0.4 fusion.19
  111.7 2.8 %collective-permute-start.2 = (bf16[4,3,48,512]{3,0,2,1:T(4,128)(2,1)S(1)}, bf16[4,3,48,512]{3,0,2,1:T(4,128)(2,1)S(1)}, u32[]{:S(2)}, u32[]{:S(2)}) collective-permute-start(bf16[4,3,48,512]{3,0,2,1:T(4,128)(2,1)S(1)} %get-tuple-element.8), channel_id=1, source_target_pairs={{112,0},{0,16},{16,32},{32,48},{48,64},{64,80},{80,96},{96,112},{1... | collective-permute-start | bytes 1769480 | tf_op jit(solution)/shard_map/ppermute | solution.py:23
  114.6 16.3 %collective-permute-done.2 = bf16[4,3,48,512]{3,0,2,1:T(4,128)(2,1)S(1)} collective-permute-done((bf16[4,3,48,512]{3,0,2,1:T(4,128)(2,1)S(1)}, bf16[4,3,48,512]{3,0,2,1:T(4,128)(2,1)S(1)}, u32[]{:S(2)}, u32[]{:S(2)}) %collective-permute-start.2) | collective-permute-done | bytes 589856 | tf_op jit(solution)/shard_map/ppermute | solution.py:23
  130.9 0.1 pad_maximum_fusion.2
  131.0 0.1 collective-permute-start.3
  131.1 2.4 %collective-permute-done.3 = bf16[4,6,6,512]{3,0,2,1:T(4,128)(2,1)S(1)} collective-permute-done((bf16[4,6,6,512]{3,0,2,1:T(4,128)(2,1)S(1)}, bf16[4,6,6,512]{3,0,2,1:T(4,128)(2,1)S(1)}, u32[]{:S(2)}, u32[]{:S(2)}) %collective-permute-start.3) | collective-permute-done | bytes 147488 | tf_op jit(solution)/shard_map/ppermute | solution.py:23
  133.5 0.8 fusion.13
  134.4 0.8 reshape.127
  135.1 1.4 copy.53
  136.5 0.0 copy-start.1
  136.5 26.6 %finish.1 = bf16[4,3,64,384]{3,2,1,0:T(8,128)(2,1)} custom-call(bf16[2,576,512]{2,1,0:T(8,128)(2,1)} %bitcast.37, bf16[512,2048]{1,0:T(8,128)(2,1)} %fc1_hbm.1, bf16[2048,512]{1,0:T(8,128)(2,1)} %fc2_hbm.1, bf16[2048,1024]{1,0:T(8,128)(2,1)} %merge_hbm.1), custom_call_target="tpu_custom_call" | custom-call | tf_op jit(solution)/shard_map/finish/pallas_call | solution.py:172
  163.1 1.9 %copy.63 = bf16[4,3,64,384]{3,2,1,0:T(8,128)(2,1)} copy(bf16[4,3,64,384]{3,2,1,0:T(8,128)(2,1)} %finish.1) | data formatting | bytes 1179648
  165.1 0.0 copy-done.1
  (5 shorter events, 0.1 us)
Async XLA Ops:
  0.0 48.8 %copy-start = (bf16[512,1536]{1,0:T(8,128)(2,1)S(1)}, bf16[512,1536]{1,0:T(8,128)(2,1)}, u32[]{:S(2)}) copy-start(bf16[512,1536]{1,0:T(8,128)(2,1)} %param.9) | copy-start | bytes 4718596
  0.0 8.4 %copy-start.4 = (s32[48]{0:T(128)S(1)}, s32[48]{0:T(128)}, u32[]{:S(2)}) copy-start(s32[48]{0:T(128)} %param.8) | copy-start | bytes 580
  1.5 18.9 %collective-permute-start = (bf16[4,3,48,512]{3,2,1,0:T(8,128)(2,1)S(1)}, bf16[4,3,48,512]{3,2,1,0:T(8,128)(2,1)S(1)}, u32[]{:S(2)}, u32[]{:S(2)}) collective-permute-start(bf16[4,3,48,512]{3,2,1,0:T(8,128)(2,1)S(1)} %get-tuple-element.11), channel_id=1, source_target_pairs={{16,0},{32,16},{48,32},{64,48},{80,64},{96,80},{112,96},{0,112},{1... | collective-permute-start | bytes 1769480 | tf_op jit(solution)/shard_map/ppermute | solution.py:23
  20.4 5.6 %collective-permute-start.1 = (bf16[4,6,6,512]{3,2,1,0:T(8,128)(2,1)S(1)}, bf16[4,6,6,512]{3,2,1,0:T(8,128)(2,1)S(1)}, u32[]{:S(2)}, u32[]{:S(2)}) collective-permute-start(bf16[4,6,6,512]{3,2,1,0:T(8,128)(2,1)S(1)} %pad_maximum_fusion.1), channel_id=1, source_target_pairs={{1,0},{2,1},{3,2},{4,3},{5,4},{6,5},{7,6},{8,7},{9,8},{10,9},{11,1... | collective-permute-start | bytes 442376 | tf_op jit(solution)/shard_map/ppermute | solution.py:23
  87.1 5.0 %copy-start.2 = (bf16[8,144,1,8,64]{1,4,3,0,2:T(8,128)(2,1)S(1)}, bf16[8,144,1,8,64]{1,4,3,0,2:T(8,128)(2,1)}, u32[]{:S(2)}) copy-start(bf16[8,144,1,8,64]{1,4,3,0,2:T(8,128)(2,1)} %copy.59) | copy-start | bytes 3538948
  99.4 3.7 %copy-start.3 = (bf16[512,512]{1,0:T(8,128)(2,1)S(1)}, bf16[512,512]{1,0:T(8,128)(2,1)}, u32[]{:S(2)}) copy-start(bf16[512,512]{1,0:T(8,128)(2,1)} %param.10) | copy-start | bytes 1572868
  111.7 19.2 %collective-permute-start.2 = (bf16[4,3,48,512]{3,0,2,1:T(4,128)(2,1)S(1)}, bf16[4,3,48,512]{3,0,2,1:T(4,128)(2,1)S(1)}, u32[]{:S(2)}, u32[]{:S(2)}) collective-permute-start(bf16[4,3,48,512]{3,0,2,1:T(4,128)(2,1)S(1)} %get-tuple-element.8), channel_id=1, source_target_pairs={{112,0},{0,16},{16,32},{32,48},{48,64},{64,80},{80,96},{96,112},{1... | collective-permute-start | bytes 1769480 | tf_op jit(solution)/shard_map/ppermute | solution.py:23
  131.0 2.5 %collective-permute-start.3 = (bf16[4,6,6,512]{3,0,2,1:T(4,128)(2,1)S(1)}, bf16[4,6,6,512]{3,0,2,1:T(4,128)(2,1)S(1)}, u32[]{:S(2)}, u32[]{:S(2)}) collective-permute-start(bf16[4,6,6,512]{3,0,2,1:T(4,128)(2,1)S(1)} %pad_maximum_fusion.2), channel_id=1, source_target_pairs={{15,0},{0,1},{1,2},{2,3},{3,4},{4,5},{5,6},{6,7},{7,8},{8,9},{9,10... | collective-permute-start | bytes 442376 | tf_op jit(solution)/shard_map/ppermute | solution.py:23
  136.5 28.6 %copy-start.1 = (bf16[512,1536]{1,0:T(8,128)(2,1)S(1)}, bf16[512,1536]{1,0:T(8,128)(2,1)}, u32[]{:S(2)}) copy-start(bf16[512,1536]{1,0:T(8,128)(2,1)} %param.9) | copy-start | bytes 4718596

commit v2 on v1

v2 whole, which is shorter than its diff:
```python
import jax
import jax.numpy as jnp
import numpy as np
from jax import lax
from jax.experimental import pallas as pl
from jax.experimental.pallas import tpu as pltpu
from jax.sharding import PartitionSpec as P

MESH = pl.DeviceIdType.MESH
BF16 = jnp.bfloat16
F32 = jnp.float32
PEERS = 16
LAT = 8
WIDTH = 512
NEVER = -1e30


def unit_row(half, unit):
    return unit if half == 0 else 5 - unit


def one_hots():
    first = np.zeros((80, 576), np.float32)
    window = np.zeros((576, 576), np.float32)
    window_edge = np.zeros((576, 80), np.float32)
    back = np.zeros((80, 144), np.float32)
    merge = np.zeros((576, 576), np.float32)
    merge_edge = np.zeros((576, 80), np.float32)

    def home(level, row, col):
        return (level * 6 + row) * 48 + col

    def merged(level, row, col):
        return (((col % 2) * 2 + row % 2) * 2 + level) * 72 + (row // 2) * 24 + col // 2

    for half in range(2):
        for unit in range(3):
            row = unit_row(half, unit)
            for level in range(2):
                for col in range(6):
                    edge = ((half * 3 + unit) * 2 + level) * 6 + col
                    first[edge, home(level, row, col)] = 1
                    back[edge, half * 72 + (unit * 2 + level) * 12 + 6 + col] = 1
                    merge_edge[merged(level, row, col), edge] = 1
                for win in range(4):
                    for col in range(12):
                        place = ((half * 4 + win) * 3 + unit) * 24 + level * 12 + col
                        at = win * 12 + 6 + col
                        if at < 48:
                            window[place, home(level, row, at)] = 1
                            merge[merged(level, row, at), place] = 1
                        else:
                            edge = ((half * 3 + unit) * 2 + level) * 6 + at - 48
                            window_edge[place, edge] = 1
    return [first, window, window_edge, back, merge, merge_edge]


ONE_HOTS = one_hots()


def dot(a, b):
    return jnp.dot(a, b, preferred_element_type=F32)


def layer_norm(values):
    average = jnp.mean(values, axis=-1, keepdims=True)
    centred = values - average
    spread = jnp.mean(centred * centred, axis=-1, keepdims=True)
    return centred * lax.rsqrt(spread + 1e-05)


def attend(block, query_at, queries, keys, bias):
    low = lax.broadcasted_iota(jnp.int32, (queries, 128), 1) < 64
    ones = jnp.ones((keys, 128), BF16)
    result = []
    for pair in range(4):
        at = 128 * pair
        query = block[pl.ds(query_at, queries), pl.ds(at, 128)] * 0.125
        query = jnp.concatenate([jnp.where(low, query, 0.0), jnp.where(low, 0.0, query)], axis=0)
        key = block[pl.ds(0, keys), pl.ds(512 + at, 128)].astype(BF16)
        value = block[pl.ds(0, keys), pl.ds(1024 + at, 128)].astype(BF16)
        scores = lax.dot_general(
            query.astype(BF16), key, (((1,), (1,)), ((), ())), preferred_element_type=F32
        )
        scores = scores + bias
        weights = jnp.exp(scores - jnp.max(scores, axis=-1, keepdims=True)).astype(BF16)
        sums = dot(weights, jnp.concatenate([value, ones], axis=1))
        mixed = sums[:, 0:128] / sums[:, 128:256]
        result.append(jnp.where(low, mixed[0:queries], mixed[queries:]))
    return result


def finish_group(restored, fc1, fc2, merge, acc):
    base = restored.astype(F32)
    normed = layer_norm(base).astype(BF16)
    part = 512

    def step(i, carry):
        cols = pl.ds(pl.multiple_of(i * part, part), part)
        pre = dot(normed, fc1[:, cols])
        hidden = (0.5 * pre * (1.0 + lax.erf(pre * 0.7071067811865476))).astype(BF16)
        acc[...] += dot(hidden, fc2[cols, :])
        return carry

    acc[...] = base
    lax.fori_loop(0, 4, step, 0)
    pieces = [acc[pl.ds(144 * i, 144), :].astype(BF16).astype(F32) for i in range(4)]
    average = sum(jnp.sum(p, axis=-1, keepdims=True) for p in pieces) / 2048
    pieces = [p - average for p in pieces]
    spread = sum(jnp.sum(p * p, axis=-1, keepdims=True) for p in pieces) / 2048
    scale = lax.rsqrt(spread + 1e-05)
    merged = None
    for i, p in enumerate(pieces):
        term = dot((p * scale).astype(BF16), merge[pl.ds(512 * i, 512), :])
        merged = term if merged is None else merged + term
    return merged


def pack_group(merged, send):
    low = lax.broadcasted_iota(jnp.int32, (72, 128), 1) < 64
    pad = jnp.zeros((8, 128), F32)
    for j in range(8):
        one = merged[0:72, 128 * j : 128 * j + 128]
        two = merged[72:144, 128 * j : 128 * j + 128]
        even = jnp.where(low, one, pltpu.roll(two, 64, 1))
        odd = jnp.where(low, pltpu.roll(one, 64, 1), two)
        send[2 * j] = jnp.concatenate([even, pad], axis=0).astype(BF16)
        send[2 * j + 1] = jnp.concatenate([odd, pad], axis=0).astype(BF16)


def unpack_group(got, out, group):
    for a in range(3):
        lines = jnp.concatenate(
            [got[s].astype(F32)[24 * a : 24 * a + 24, :] for s in range(PEERS)], axis=0
        )
        turned = lines.T
        out[2 * group, a] = turned[0:64, :].astype(BF16)
        out[2 * group + 1, a] = turned[64:128, :].astype(BF16)


def kernel(
    tokens_hbm, first_hbm, window_hbm, window_edge_hbm, back_hbm, merge_order_hbm, merge_edge_hbm,
    qkv_hbm, proj_hbm, fc1_hbm, fc2_hbm, merge_hbm, bias_own, bias_rim, flags,
    out,
    tokens, first, window, window_edge, back, merge_order, merge_edge,
    qkv, proj, fc1, fc2, merge,
    edge_out, edge_in, ordered, rim_out, rim_in, far_out, far_in, packed, mixed, updated,
    back_out, back_in, acc, send, got,
    token_sem, load_sem, edge_sem, rim_sem, far_sem, back_sem, send_sem, recv_sem, own_sem,
):
    sources = [
        first_hbm, window_hbm, window_edge_hbm, qkv_hbm, proj_hbm, back_hbm, merge_order_hbm,
        merge_edge_hbm, fc1_hbm, fc2_hbm, merge_hbm,
    ]
    places = [
        first, window, window_edge, qkv, proj, back, merge_order, merge_edge, fc1, fc2, merge,
    ]
    token_loads = [
        pltpu.make_async_copy(tokens_hbm.at[pl.ds(576 * g, 576)], tokens.at[g], token_sem.at[g])
        for g in range(2)
    ]
    loads = [
        pltpu.make_async_copy(src, dst, load_sem.at[i])
        for i, (src, dst) in enumerate(zip(sources, places))
    ]
    token_loads[0].start()
    loads[0].start()
    token_loads[1].start()
    for load in loads[1:]:
        load.start()

    lat = lax.axis_index("lat")
    lon = lax.axis_index("lon")
    up = {"lat": lax.rem(lat + LAT - 1, LAT)}
    down = {"lat": lax.rem(lat + 1, LAT)}
    west = {"lon": lax.rem(lon + PEERS - 1, PEERS)}
    east = {"lon": lax.rem(lon + 1, PEERS)}
    barrier = pltpu.get_barrier_semaphore()
    for d in range(1, PEERS):
        pl.semaphore_signal(
            barrier, inc=1, device_id={"lon": lax.rem(lon + d, PEERS)}, device_id_type=MESH
        )
    for to in (up, down):
        pl.semaphore_signal(barrier, inc=1, device_id=to, device_id_type=MESH)
    pl.semaphore_wait(barrier, PEERS + 1)

    def remote(src, dst, sems, where, to):
        copy = pltpu.make_async_remote_copy(
            src_ref=src, dst_ref=dst, send_sem=sems.at[(0,) + where], recv_sem=sems.at[(1,) + where],
            device_id=to, device_id_type=MESH,
        )
        copy.start()
        return copy

    edges = []
    for g in range(2):
        token_loads[g].wait()
        if g == 0:
            loads[0].wait()
        edge_out[g] = dot(first[...], tokens[g]).astype(BF16)
        edges.append(remote(edge_out.at[g], edge_in.at[g], edge_sem, (g,), west))
    for load in loads[1:3]:
        load.wait()
    rims = []
    for g in range(2):
        inner = dot(window[...], tokens[g])
        edges[g].wait_recv()
        placed = inner + dot(window_edge[...], edge_in[g])
        ordered[g] = placed.astype(BF16)
        for half in range(2):
            rim_out[g, half] = jnp.concatenate(
                [placed[288 * half + 72 * w : 288 * half + 72 * w + 24] for w in range(4)], axis=0
            ).astype(BF16)
            far_out[g, half] = jnp.concatenate(
                [placed[288 * half + 72 * w + 24 : 288 * half + 72 * w + 48] for w in range(4)], axis=0
            ).astype(BF16)
            rims.append(
                remote(rim_out.at[g, half], rim_in.at[g, 1 - half], rim_sem, (g, half), (up, down)[half])
            )
    loads[3].wait()
    for g in range(2):
        normed = layer_norm(ordered[g].astype(F32)).astype(BF16)
        for part in range(3):
            cols = pl.ds(512 * part, 512)
            result = dot(normed, qkv[:, cols])
            for k in range(8):
                packed[g, k, pl.ds(0, 72), cols] = result[72 * k : 72 * k + 72]
        for k in range(8):
            packed[g, k, pl.ds(120, 8), :] = jnp.zeros((8, 1536), F32)
    fars = []
    for g in range(2):
        for half in range(2):
            rims[2 * g + half].wait_recv()
        rim = rim_in[g].reshape(192, WIDTH)
        normed = layer_norm(rim.astype(F32)).astype(BF16)
        for part in range(3):
            cols = pl.ds(512 * part, 512)
            result = dot(normed, qkv[:, cols])
            for k in range(8):
                packed[g, k, pl.ds(72, 24), cols] = result[24 * k : 24 * k + 24]

        def rim_step(k, carry, g=g):
            parts = attend(packed.at[g, k], 72, 24, 96, bias_rim[k // 4])
            for pair in range(4):
                mixed[g, pl.ds(pl.multiple_of(k * 72, 8), 24), pl.ds(128 * pair, 128)] = parts[pair]
            return carry

        lax.fori_loop(0, 8, rim_step, 0)
        for half in range(2):
            seen = jnp.concatenate(
                [mixed[g, pl.ds(288 * half + 72 * w, 24), :] for w in range(4)], axis=0
            )
            far_out[g, half] = jnp.where(
                flags[pl.ds(half, 1), :] > 0, seen, far_out[g, half].astype(F32)
            ).astype(BF16)
            fars.append(
                remote(far_out.at[g, half], far_in.at[g, 1 - half], far_sem, (g, half), (up, down)[half])
            )
    loads[4].wait()
    loads[5].wait()
    copies = []
    backs = []
    for g in range(2):
        for half in range(2):
            fars[2 * g + half].wait_recv()
        far = far_in[g].reshape(192, WIDTH)
        normed = layer_norm(far.astype(F32)).astype(BF16)
        for part in range(1, 3):
            cols = pl.ds(512 * part, 512)
            result = dot(normed, qkv[:, cols])
            for k in range(8):
                packed[g, k, pl.ds(96, 24), cols] = result[24 * k : 24 * k + 24]

        def own_step(k, carry, g=g):
            parts = attend(packed.at[g, k], 0, 72, 128, bias_own[k // 4])
            for pair in range(4):
                mixed[g, pl.ds(pl.multiple_of(k * 72, 8), 72), pl.ds(128 * pair, 128)] = parts[pair]
            return carry

        lax.fori_loop(0, 8, own_step, 0)
        for half in range(2):
            final = far_in[g, half].astype(F32)
            for w in range(4):
                rows = pl.ds(288 * half + 72 * w, 24)
                mixed[g, rows, :] = jnp.where(
                    flags[pl.ds(2 + half, 1), :] > 0, final[24 * w : 24 * w + 24], mixed[g, rows, :]
                )
        fresh = ordered[g].astype(F32) + dot(mixed[g].astype(BF16), proj[...])
        updated[g] = fresh.astype(BF16)
        rim = jnp.concatenate([fresh[216:288], fresh[504:576]], axis=0).astype(BF16)
        back_out[g] = dot(back[...], rim).astype(BF16)
        backs.append(remote(back_out.at[g], back_in.at[g], back_sem, (g,), east))
        if g == 0:
            for load in loads[6:]:
                load.wait()
        inner = dot(merge_order[...], updated[g])
        backs[g].wait_recv()
        restored = (inner + dot(merge_edge[...], back_in[g])).astype(BF16)
        merged = finish_group(restored, fc1, fc2, merge, acc)
        pack_group(merged, send.at[g])
        for d in range(1, PEERS):
            to = lax.rem(lon + d, PEERS)
            copy = pltpu.make_async_remote_copy(
                src_ref=send.at[g, to], dst_ref=got.at[g, lon],
                send_sem=send_sem.at[g, d], recv_sem=recv_sem.at[g, d],
                device_id={"lon": to}, device_id_type=MESH,
            )
            copy.start()
            copies.append(copy)
        own = pltpu.make_async_copy(send.at[g, lon], got.at[g, lon], own_sem.at[g])
        own.start()
        copies.append(own)
    for g in range(2):
        for copy in copies[16 * g : 16 * g + 16]:
            copy.wait()
        unpack_group(got.at[g], out, g)
    for copy in edges + rims + fars + backs:
        copy.wait_send()


def body(tokens, band_ids, qkv_weight, proj_weight, fc1_weight, fc2_weight, merge_weight):
    constants = [jnp.asarray(m, BF16) for m in ONE_HOTS]
    start = lax.axis_index("lat") * 6
    around = lax.dynamic_slice_in_dim(jnp.concatenate([band_ids[45:], band_ids, band_ids[:3]]), start, 12)
    bias_own, bias_rim, edge_out, edge_in = [], [], [], []
    for half in range(2):
        units = [unit_row(half, u) for u in range(3)] + ([-1, -2, -3] if half == 0 else [6, 7, 8])
        band = [around[u + 3] for u in units]
        key = jnp.concatenate([jnp.stack(band[:5]).repeat(24), jnp.full((8,), -1, jnp.int32)])
        bias = jnp.where(key[:, None] == key[None, :], 0.0, NEVER).astype(F32)
        bias_own.append(jnp.concatenate([bias[:72], bias[:72]], axis=0))
        bias_rim.append(jnp.concatenate([bias[72:96, :96], bias[72:96, :96]], axis=0))
        edge_out.append(band[2] == band[3])
        edge_in.append(band[0] == band[5])
    flags = jnp.broadcast_to(jnp.stack(edge_out + edge_in)[:, None].astype(F32), (4, WIDTH))
    hbm = pl.BlockSpec(memory_space=pl.ANY)
    vmem = pl.BlockSpec(memory_space=pltpu.VMEM)
    dma = pltpu.SemaphoreType.DMA
    return pl.pallas_call(
        kernel,
        out_shape=jax.ShapeDtypeStruct((4, 3, 64, 384), BF16),
        in_specs=[hbm] * 12 + [vmem] * 3,
        out_specs=vmem,
        scratch_shapes=[
            pltpu.VMEM((2, 576, WIDTH), BF16),
            pltpu.VMEM((80, 576), BF16),
            pltpu.VMEM((576, 576), BF16),
            pltpu.VMEM((576, 80), BF16),
            pltpu.VMEM((80, 144), BF16),
            pltpu.VMEM((576, 576), BF16),
            pltpu.VMEM((576, 80), BF16),
            pltpu.VMEM((512, 1536), BF16),
            pltpu.VMEM((512, 512), BF16),
            pltpu.VMEM((512, 2048), BF16),
            pltpu.VMEM((2048, 512), BF16),
            pltpu.VMEM((2048, 1024), BF16),
            pltpu.VMEM((2, 80, WIDTH), BF16),
            pltpu.VMEM((2, 80, WIDTH), BF16),
            pltpu.VMEM((2, 576, WIDTH), BF16),
            pltpu.VMEM((2, 2, 96, WIDTH), BF16),
            pltpu.VMEM((2, 2, 96, WIDTH), BF16),
            pltpu.VMEM((2, 2, 96, WIDTH), BF16),
            pltpu.VMEM((2, 2, 96, WIDTH), BF16),
            pltpu.VMEM((2, 8, 128, 1536), F32),
            pltpu.VMEM((2, 576, WIDTH), F32),
            pltpu.VMEM((2, 576, WIDTH), BF16),
            pltpu.VMEM((2, 80, WIDTH), BF16),
            pltpu.VMEM((2, 80, WIDTH), BF16),
            pltpu.VMEM((576, WIDTH), F32),
            pltpu.VMEM((2, PEERS, 80, 128), BF16),
            pltpu.VMEM((2, PEERS, 80, 128), BF16),
            dma((2,)),
            dma((11,)),
            dma((2, 2)),
            dma((2, 2, 2)),
            dma((2, 2, 2)),
            dma((2, 2)),
            dma((2, PEERS)),
            dma((2, PEERS)),
            dma((2,)),
        ],
        compiler_params=pltpu.CompilerParams(
            collective_id=0, has_side_effects=True, vmem_limit_bytes=56 * 1024 * 1024
        ),
        name="layer",
    )(
        tokens.reshape(4 * 6 * 48, WIDTH), *constants,
        qkv_weight, proj_weight, fc1_weight, fc2_weight, merge_weight,
        jnp.stack(bias_own), jnp.stack(bias_rim), flags,
    )


def solution(mesh):
    placed = (P(None, "lat", "lon", None), P(), P(), P(), P(), P(), P())
    return jax.shard_map(
        body, mesh=mesh, in_specs=placed, out_specs=P(None, "lat", "lon", None), check_vma=False
    )
```

time: 166 us -> 92.9 us (0.56)
  local copies, waits for them, and re-layouts: 63.9 us -> 4.63 us
  Pallas kernels: 26.6 us -> 77.3 us
  waiting for transfers between devices: 34 us -> 0 us
  matrix products: 16.3 us -> 0 us
  starting transfers between devices: 11.5 us -> 0 us
  other arithmetic: 12.5 us -> 5.54 us
  between operations: 0.2 us -> 5.16 us
    pallas_call x1, Pallas kernels: 26.6 us -> 77.3 us  [body(): pl.pallas_call(kernel, out_shape=jax.ShapeDtypeStruct((4, 3, 64, 384), BF...]
    ppermute x4 -> x0, waiting for transfers between devices: 34 us -> none  [shifted_2(): return lax.ppermute(block, axis, route)]
    convert_element_type x5 -> x0, local copies, waits for them, and re-layouts: 17.8 us -> none  [the longest x4 15.2 us: window_attention(): ordered.astype(jnp.float32)]
    reshape x5 -> x2, local copies, waits for them, and re-layouts: 17.5 us -> 0.16 us  [body(): jnp.stack(band[:5]).repeat(24)]
    dot_general x4 -> x0, matrix products: 16.3 us -> none  [the longest x1 5.52 us: window_attention(): jnp.dot(normed, qkv_weight, preferred_element_type=jnp.float32)]
    unnamed x14 -> x1, local copies, waits for them, and re-layouts: 15.5 us -> 1.94 us
    ppermute x4 -> x0, starting transfers between devices: 11.5 us -> none  [shifted_2(): return lax.ppermute(block, axis, route)]
    slice x3 -> x8, local copies, waits for them, and re-layouts: 8.01 us -> 1.64 us  [the longest x3 0.82 us: body(): band = [around[u + 3] for u in units]]
  transfers between devices with their start and end apart: 4 -> 0, of which waited for: 4 -> 0; matrix products, arithmetic and copies ran while one was open for 0% -> 0% of each run, Pallas kernels for 0% -> 0%
where the time goes in v2:
time: 92.9 us; the launch traced here: 92.6 us
  Pallas kernels  77.3 us (83%)
  other arithmetic  5.54 us (6%)
  between operations  5.16 us (6%)
  local copies, waits for them, and re-layouts  4.63 us (5%)
    pallas_call x1, Pallas kernels, body(): pl.pallas_call(kernel, out_shape=jax.ShapeDtypeStruct((4, 3, 64, 384), BF...  77.3 us
    another operation x1, other arithmetic, body(): jnp.stack(band[:5]).repeat(24)  3.26 us
    unnamed x1, local copies, waits for them, and re-layouts  1.94 us

profile of v2, /device:TPU:1, one launch (start us, length us, event | category | flops | bytes accessed | tf_op | source)
XLA Modules:
  0.0 92.6 jit_solution(14465245635784057428)
XLA Ops:
  0.0 0.8 fusion.1
  0.8 0.7 pad_add_fusion
  1.5 0.1 dynamic_slice.3
  1.6 0.1 slice.69
  1.7 0.1 slice.62
  1.8 0.7 fusion
  7.5 3.3 %pad_add_fusion.1 = (s32[5]{0:T(128)S(1)}, s32[5]{0:T(128)S(1)}) fusion(s32[1]{0:T(128)} %get-tuple-element.13, s32[1]{0:T(128)} %get-tuple-element.14, s32[3]{0:T(128)S(1)} %slice.62, s32[2]{0:T(128)S(1)} %slice.69, s32[1]{0:T(128)} %get-tuple-element.10, s32[1]{0:T(128)} %get-tuple-element.11, s32[1]{0:T(128)} %get-tuple-element.12), kind=kLoop, calls=%fused_computation.10 | loop fusion | flops 25 | bytes 80 | tf_op jit(solution)/shard_map/stack | solution.py:329
  10.8 0.1 add_convert_fusion
  10.8 0.1 broadcast_in_dim.26
  10.9 0.1 reshape.56
  11.0 0.1 broadcast_in_dim.29
  11.1 0.1 reshape.57
  11.2 0.7 broadcast_in_dim.30.flags
  11.8 0.1 compare_select_fusion
  12.0 0.1 compare_select_fusion.1
  12.1 0.6 pad_maximum_fusion.1.bias_rim
  12.7 0.7 pad_maximum_fusion.bias_own
  13.4 77.3 %layer.1 = bf16[4,3,64,384]{3,2,1,0:T(8,128)(2,1)} custom-call(bf16[1152,512]{1,0:T(8,128)(2,1)} %bitcast.9, bf16[80,576]{1,0:T(8,128)(2,1)} %constant.30.clone.first_hbm, bf16[576,576]{1,0:T(8,128)(2,1)} %constant.31.clone.window_hbm, bf16[576,80]{1,0:T(8,128)(2,1)} %constant.32.clone.window_edge_hbm, bf16[80,144]{1,0:T(8,128)(2,1)} %constant.33.clone.back_hbm, ...), custom_call_target="tpu_custom_call" | custom-call | tf_op jit(solution)/shard_map/layer/pallas_call | solution.py:339
  90.7 1.9 %copy.15 = bf16[4,3,64,384]{3,2,1,0:T(8,128)(2,1)} copy(bf16[4,3,64,384]{3,2,1,0:T(8,128)(2,1)} %layer.1) | data formatting | bytes 1179648
  (10 shorter events, 0.1 us)

commit v3 on v2

v3 whole, which is shorter than its diff:
```python
import jax
import jax.numpy as jnp
from jax import lax
from jax.experimental import pallas as pl
from jax.experimental.pallas import tpu as pltpu
from jax.sharding import PartitionSpec as P

MESH = pl.DeviceIdType.MESH
BF16 = jnp.bfloat16
F32 = jnp.float32
PEERS = 16
LAT = 8
WIDTH = 512
NEVER = -1e30


def unit_row(half, unit):
    return unit if half == 0 else 5 - unit


def split(index, size):
    whole = jnp.floor((index + 0.5) * (1.0 / size))
    return whole, index - whole * size


def one_hot(picks, width):
    lane = lax.broadcasted_iota(jnp.int32, picks.shape, 1).astype(F32)
    tiles = [jnp.where(lane + at == picks, 1.0, 0.0) for at in range(0, width, 128)]
    return jnp.concatenate(tiles, axis=1)[:, 0:width].astype(BF16)


def index_of(rows):
    return lax.broadcasted_iota(jnp.int32, (rows, 128), 0).astype(F32)


def edge_picks():
    index = index_of(80)
    half, rest = split(index, 36)
    unit, rest = split(rest, 12)
    level, col = split(rest, 6)
    row = unit + half * (5 - 2 * unit)
    real = index < 72
    first = jnp.where(real, (level * 6 + row) * 48 + col, -1.0)
    back = jnp.where(real, half * 72 + (unit * 2 + level) * 12 + 6 + col, -1.0)
    return first, back


def window_picks():
    half, rest = split(index_of(576), 288)
    win, rest = split(rest, 72)
    unit, rest = split(rest, 24)
    level, col = split(rest, 12)
    row = unit + half * (5 - 2 * unit)
    at = win * 12 + 6 + col
    here = at < 48
    inner = jnp.where(here, (level * 6 + row) * 48 + at, -1.0)
    edge = jnp.where(here, -1.0, ((half * 3 + unit) * 2 + level) * 6 + at - 48)
    return inner, edge


def merge_picks():
    parity, rest = split(index_of(576), 144)
    col_parity, row_parity = split(parity, 2)
    level, rest = split(rest, 72)
    a, b = split(rest, 24)
    row = 2 * a + row_parity
    col = 2 * b + col_parity
    half = jnp.where(row > 2.5, 1.0, 0.0)
    unit = row + half * (5 - 2 * row)
    win, at = split(col - 6, 12)
    here = col > 5.5
    inner = jnp.where(here, ((half * 4 + win) * 3 + unit) * 24 + level * 12 + at, -1.0)
    edge = jnp.where(here, -1.0, ((half * 3 + unit) * 2 + level) * 6 + col)
    return inner, edge


def dot(a, b):
    return jnp.dot(a, b, preferred_element_type=F32)


def layer_norm(values):
    average = jnp.mean(values, axis=-1, keepdims=True)
    centred = values - average
    spread = jnp.mean(centred * centred, axis=-1, keepdims=True)
    return centred * lax.rsqrt(spread + 1e-05)


def attend(block, query_at, bias):
    head = lax.broadcasted_iota(jnp.int32, (48, 256), 1) // 64
    result = []
    for quad in range(2):
        at = 256 * quad
        query = block[pl.ds(query_at, 48), pl.ds(at, 256)] * 0.125
        query = jnp.concatenate([jnp.where(head == h, query, 0.0) for h in range(4)], axis=0)
        key = block[:, pl.ds(512 + at, 256)].astype(BF16)
        value = block[:, pl.ds(1024 + at, 256)].astype(BF16)
        scores = lax.dot_general(
            query.astype(BF16), key, (((1,), (1,)), ((), ())), preferred_element_type=F32
        )
        scores = scores + bias
        weights = jnp.exp(scores - jnp.max(scores, axis=-1, keepdims=True))
        total = jnp.sum(weights, axis=-1, keepdims=True)
        mixed = dot(weights.astype(BF16), value) / total
        picked = mixed[0:48]
        for h in range(1, 4):
            picked = jnp.where(head == h, mixed[48 * h : 48 * h + 48], picked)
        result.append(picked)
    return result


def band_biases(band_ids, lat, bias_own, bias_rim):
    seen, final = [], []
    for half in range(2):
        units = [unit_row(half, u) for u in range(3)] + ([-1, -2, -3] if half == 0 else [6, 7, 8])
        band = [band_ids[lax.rem(lat * 6 + u + 48, 48)] for u in units]

        def band_of(shape, dim):
            unit = lax.broadcasted_iota(jnp.int32, shape, dim) // 24
            held = jnp.full(shape, -1, jnp.int32)
            for u in range(5):
                held = jnp.where(unit == u, band[u], held)
            return held

        bias = jnp.where(band_of((96, 128), 0) == band_of((96, 128), 1), 0.0, NEVER)
        near = lax.broadcasted_iota(jnp.int32, (48, 128), 1) < 96
        for head in range(4):
            bias_own[half, pl.ds(48 * head, 48), :] = bias[0:48]
            bias_rim[half, pl.ds(48 * head, 48), :] = jnp.where(near, bias[48:96], NEVER)
        seen.append(jnp.full((1, WIDTH), band[2], jnp.int32) == band[3])
        final.append(jnp.full((1, WIDTH), band[0], jnp.int32) == band[5])
    return seen, final


def finish_group(restored, fc1, fc2, merge, acc):
    base = restored.astype(F32)
    normed = layer_norm(base).astype(BF16)
    hidden = []
    for i in range(4):
        pre = dot(normed, fc1[:, pl.ds(512 * i, 512)])
        hidden.append((0.5 * pre * (1.0 + lax.erf(pre * 0.7071067811865476))).astype(BF16))
    acc[...] = base + dot(jnp.concatenate(hidden, axis=1), fc2[...])
    pieces = [acc[pl.ds(144 * i, 144), :].astype(BF16).astype(F32) for i in range(4)]
    average = sum(jnp.sum(p, axis=-1, keepdims=True) for p in pieces) / 2048
    pieces = [p - average for p in pieces]
    spread = sum(jnp.sum(p * p, axis=-1, keepdims=True) for p in pieces) / 2048
    scale = lax.rsqrt(spread + 1e-05)
    merged = None
    for i, p in enumerate(pieces):
        term = dot((p * scale).astype(BF16), merge[pl.ds(512 * i, 512), :])
        merged = term if merged is None else merged + term
    return merged


def pack_group(merged, send):
    low = lax.broadcasted_iota(jnp.int32, (72, 128), 1) < 64
    pad = jnp.zeros((8, 128), F32)
    for j in range(8):
        one = merged[0:72, 128 * j : 128 * j + 128]
        two = merged[72:144, 128 * j : 128 * j + 128]
        even = jnp.where(low, one, pltpu.roll(two, 64, 1))
        odd = jnp.where(low, pltpu.roll(one, 64, 1), two)
        send[2 * j] = jnp.concatenate([even, pad], axis=0).astype(BF16)
        send[2 * j + 1] = jnp.concatenate([odd, pad], axis=0).astype(BF16)


def unpack_group(got, out, group):
    for a in range(3):
        lines = jnp.concatenate(
            [got[s].astype(F32)[24 * a : 24 * a + 24, :] for s in range(PEERS)], axis=0
        )
        turned = lines.T
        out[2 * group, a] = turned[0:64, :].astype(BF16)
        out[2 * group + 1, a] = turned[64:128, :].astype(BF16)


def kernel(
    tokens_hbm, qkv_hbm, proj_hbm, fc1_hbm, fc2_hbm, merge_hbm, band_ids,
    out,
    tokens, first, window, window_edge, back, merge_order, merge_edge,
    qkv, proj, fc1, fc2, merge,
    edge_out, edge_in, ordered, rim_out, rim_in, far_out, far_in, packed, mixed, updated,
    back_out, back_in, acc, send, got, bias_own, bias_rim, rim_mixed,
    token_sem, load_sem, edge_sem, rim_sem, far_sem, back_sem, send_sem, recv_sem, own_sem,
):
    sources = [qkv_hbm, proj_hbm, fc1_hbm, fc2_hbm, merge_hbm]
    places = [qkv, proj, fc1, fc2, merge]
    token_loads = [
        pltpu.make_async_copy(tokens_hbm.at[pl.ds(576 * g, 576)], tokens.at[g], token_sem.at[g])
        for g in range(2)
    ]
    loads = [
        pltpu.make_async_copy(src, dst, load_sem.at[i])
        for i, (src, dst) in enumerate(zip(sources, places))
    ]
    for load in token_loads + loads:
        load.start()

    lat = lax.axis_index("lat")
    lon = lax.axis_index("lon")
    up = {"lat": lax.rem(lat + LAT - 1, LAT)}
    down = {"lat": lax.rem(lat + 1, LAT)}
    west = {"lon": lax.rem(lon + PEERS - 1, PEERS)}
    east = {"lon": lax.rem(lon + 1, PEERS)}
    barrier = pltpu.get_barrier_semaphore()
    for d in range(1, PEERS):
        pl.semaphore_signal(
            barrier, inc=1, device_id={"lon": lax.rem(lon + d, PEERS)}, device_id_type=MESH
        )
    for to in (up, down):
        pl.semaphore_signal(barrier, inc=1, device_id=to, device_id_type=MESH)
    picks, back_picks = edge_picks()
    first[...] = one_hot(picks, 576)
    back[...] = one_hot(back_picks, 144)
    picks, far_picks = window_picks()
    window[...] = one_hot(picks, 576)
    window_edge[...] = one_hot(far_picks, 80)
    pl.semaphore_wait(barrier, PEERS + 1)

    def remote(src, dst, sems, where, to):
        copy = pltpu.make_async_remote_copy(
            src_ref=src, dst_ref=dst, send_sem=sems.at[(0,) + where], recv_sem=sems.at[(1,) + where],
            device_id=to, device_id_type=MESH,
        )
        copy.start()
        return copy

    edges = []
    for g in range(2):
        token_loads[g].wait()
        edge_out[g] = dot(first[...], tokens[g]).astype(BF16)
        edges.append(remote(edge_out.at[g], edge_in.at[g], edge_sem, (g,), west))
    rims = []
    for g in range(2):
        inner = dot(window[...], tokens[g])
        edges[g].wait_recv()
        placed = inner + dot(window_edge[...], edge_in[g])
        ordered[g] = placed.astype(BF16)
        for half in range(2):
            rim_out[g, half] = jnp.concatenate(
                [placed[288 * half + 72 * w : 288 * half + 72 * w + 24] for w in range(4)], axis=0
            ).astype(BF16)
            far_out[g, half] = jnp.concatenate(
                [placed[288 * half + 72 * w + 24 : 288 * half + 72 * w + 48] for w in range(4)], axis=0
            ).astype(BF16)
            rims.append(
                remote(rim_out.at[g, half], rim_in.at[g, 1 - half], rim_sem, (g, half), (up, down)[half])
            )
    picks, far_picks = merge_picks()
    merge_order[...] = one_hot(picks, 576)
    merge_edge[...] = one_hot(far_picks, 80)
    edge_seen, edge_final = band_biases(band_ids, lat, bias_own, bias_rim)
    loads[0].wait()
    for g in range(2):
        normed = layer_norm(ordered[g].astype(F32)).astype(BF16)
        for part in range(3):
            cols = pl.ds(512 * part, 512)
            result = dot(normed, qkv[:, cols])
            for k in range(8):
                packed[g, k, pl.ds(0, 72), cols] = result[72 * k : 72 * k + 72]
        for k in range(8):
            packed[g, k, pl.ds(96, 32), :] = jnp.zeros((32, 1536), F32)
    fars = []
    for g in range(2):
        for half in range(2):
            rims[2 * g + half].wait_recv()
        rim = rim_in[g].reshape(192, WIDTH)
        normed = layer_norm(rim.astype(F32)).astype(BF16)
        for part in range(3):
            cols = pl.ds(512 * part, 512)
            result = dot(normed, qkv[:, cols])
            for k in range(8):
                packed[g, k, pl.ds(72, 24), cols] = result[24 * k : 24 * k + 24]

        for k in range(8):
            parts = attend(packed.at[g, k], 48, bias_rim[k // 4])
            for quad in range(2):
                cols = pl.ds(256 * quad, 256)
                mixed[g, pl.ds(72 * k + 48, 24), cols] = parts[quad][0:24]
                rim_mixed[g, pl.ds(24 * k, 24), cols] = parts[quad][24:48]
        for half in range(2):
            seen = rim_mixed[g, pl.ds(96 * half, 96), :]
            far_out[g, half] = jnp.where(
                edge_seen[half], seen, far_out[g, half].astype(F32)
            ).astype(BF16)
            fars.append(
                remote(far_out.at[g, half], far_in.at[g, 1 - half], far_sem, (g, half), (up, down)[half])
            )
    loads[1].wait()
    copies = []
    backs = []
    for g in range(2):
        for half in range(2):
            fars[2 * g + half].wait_recv()
        far = far_in[g].reshape(192, WIDTH)
        normed = layer_norm(far.astype(F32)).astype(BF16)
        for part in range(1, 3):
            cols = pl.ds(512 * part, 512)
            result = dot(normed, qkv[:, cols])
            for k in range(8):
                packed[g, k, pl.ds(96, 24), cols] = result[24 * k : 24 * k + 24]

        for k in range(8):
            parts = attend(packed.at[g, k], 0, bias_own[k // 4])
            for quad in range(2):
                mixed[g, pl.ds(72 * k, 48), pl.ds(256 * quad, 256)] = parts[quad]
        for half in range(2):
            final = far_in[g, half].astype(F32)
            for w in range(4):
                rows = pl.ds(288 * half + 72 * w, 24)
                mixed[g, rows, :] = jnp.where(
                    edge_final[half], final[24 * w : 24 * w + 24], mixed[g, rows, :]
                )
        fresh = ordered[g].astype(F32) + dot(mixed[g].astype(BF16), proj[...])
        updated[g] = fresh.astype(BF16)
        rim = jnp.concatenate([fresh[216:288], fresh[504:576]], axis=0).astype(BF16)
        back_out[g] = dot(back[...], rim).astype(BF16)
        backs.append(remote(back_out.at[g], back_in.at[g], back_sem, (g,), east))
        if g == 0:
            for load in loads[2:]:
                load.wait()
        inner = dot(merge_order[...], updated[g])
        backs[g].wait_recv()
        restored = (inner + dot(merge_edge[...], back_in[g])).astype(BF16)
        merged = finish_group(restored, fc1, fc2, merge, acc)
        pack_group(merged, send.at[g])
        for d in range(1, PEERS):
            to = lax.rem(lon + d, PEERS)
            copy = pltpu.make_async_remote_copy(
                src_ref=send.at[g, to], dst_ref=got.at[g, lon],
                send_sem=send_sem.at[g, d], recv_sem=recv_sem.at[g, d],
                device_id={"lon": to}, device_id_type=MESH,
            )
            copy.start()
            copies.append(copy)
        own = pltpu.make_async_copy(send.at[g, lon], got.at[g, lon], own_sem.at[g])
        own.start()
        copies.append(own)
    for g in range(2):
        for copy in copies[16 * g : 16 * g + 16]:
            copy.wait()
        unpack_group(got.at[g], out, g)
    for copy in edges + rims + fars + backs:
        copy.wait_send()


def body(tokens, band_ids, qkv_weight, proj_weight, fc1_weight, fc2_weight, merge_weight):
    hbm = pl.BlockSpec(memory_space=pl.ANY)
    vmem = pl.BlockSpec(memory_space=pltpu.VMEM)
    dma = pltpu.SemaphoreType.DMA
    return pl.pallas_call(
        kernel,
        out_shape=jax.ShapeDtypeStruct((4, 3, 64, 384), BF16),
        in_specs=[hbm] * 6 + [pl.BlockSpec(memory_space=pltpu.SMEM)],
        out_specs=vmem,
        scratch_shapes=[
            pltpu.VMEM((2, 576, WIDTH), BF16),
            pltpu.VMEM((80, 576), BF16),
            pltpu.VMEM((576, 576), BF16),
            pltpu.VMEM((576, 80), BF16),
            pltpu.VMEM((80, 144), BF16),
            pltpu.VMEM((576, 576), BF16),
            pltpu.VMEM((576, 80), BF16),
            pltpu.VMEM((512, 1536), BF16),
            pltpu.VMEM((512, 512), BF16),
            pltpu.VMEM((512, 2048), BF16),
            pltpu.VMEM((2048, 512), BF16),
            pltpu.VMEM((2048, 1024), BF16),
            pltpu.VMEM((2, 80, WIDTH), BF16),
            pltpu.VMEM((2, 80, WIDTH), BF16),
            pltpu.VMEM((2, 576, WIDTH), BF16),
            pltpu.VMEM((2, 2, 96, WIDTH), BF16),
            pltpu.VMEM((2, 2, 96, WIDTH), BF16),
            pltpu.VMEM((2, 2, 96, WIDTH), BF16),
            pltpu.VMEM((2, 2, 96, WIDTH), BF16),
            pltpu.VMEM((2, 8, 128, 1536), F32),
            pltpu.VMEM((2, 576, WIDTH), F32),
            pltpu.VMEM((2, 576, WIDTH), BF16),
            pltpu.VMEM((2, 80, WIDTH), BF16),
            pltpu.VMEM((2, 80, WIDTH), BF16),
            pltpu.VMEM((576, WIDTH), F32),
            pltpu.VMEM((2, PEERS, 80, 128), BF16),
            pltpu.VMEM((2, PEERS, 80, 128), BF16),
            pltpu.VMEM((2, 192, 128), F32),
            pltpu.VMEM((2, 192, 128), F32),
            pltpu.VMEM((2, 192, WIDTH), F32),
            dma((2,)),
            dma((5,)),
            dma((2, 2)),
            dma((2, 2, 2)),
            dma((2, 2, 2)),
            dma((2, 2)),
            dma((2, PEERS)),
            dma((2, PEERS)),
            dma((2,)),
        ],
        compiler_params=pltpu.CompilerParams(
            collective_id=0, has_side_effects=True, vmem_limit_bytes=56 * 1024 * 1024
        ),
        name="layer",
    )(
        tokens.reshape(4 * 6 * 48, WIDTH),
        qkv_weight, proj_weight, fc1_weight, fc2_weight, merge_weight, band_ids,
    )


def solution(mesh):
    placed = (P(None, "lat", "lon", None), P(), P(), P(), P(), P(), P())
    return jax.shard_map(
        body, mesh=mesh, in_specs=placed, out_specs=P(None, "lat", "lon", None), check_vma=False
    )
```

time: 92.9 us -> 58.9 us (0.63)
  Pallas kernels: 77.3 us -> 56.8 us
  other arithmetic: 5.54 us -> 0 us
  between operations: 5.16 us -> 0.01 us
  local copies, waits for them, and re-layouts: 4.63 us -> 1.94 us
    pallas_call x1, Pallas kernels: 77.3 us -> 56.8 us  [body(): pl.pallas_call(kernel, out_shape=jax.ShapeDtypeStruct((4, 3, 64, 384), BF...]
    another operation x7 -> x0, other arithmetic: 4.57 us -> none  [the longest x1 3.26 us: body(): jnp.stack(band[:5]).repeat(24)]
    slice x8 -> x0, local copies, waits for them, and re-layouts: 1.64 us -> none  [the longest x3 0.82 us: body(): band = [around[u + 3] for u in units]]
where the time goes in v3:
time: 58.9 us; the launch traced here: 58.8 us
  Pallas kernels  56.8 us (96%)
  local copies, waits for them, and re-layouts  1.94 us (3%)
    pallas_call x1, Pallas kernels, body(): pl.pallas_call(kernel, out_shape=jax.ShapeDtypeStruct((4, 3, 64, 384), BF...  56.8 us
    unnamed x1, local copies, waits for them, and re-layouts  1.94 us

profile of v3, /device:TPU:1, one launch (start us, length us, event | category | flops | bytes accessed | tf_op | source)
XLA Modules:
  0.0 58.8 jit_solution(16187702978168964036)
XLA Ops:
  0.0 56.8 %layer.1 = bf16[4,3,64,384]{3,2,1,0:T(8,128)(2,1)} custom-call(bf16[1152,512]{1,0:T(8,128)(2,1)} %bitcast.1, bf16[512,1536]{1,0:T(8,128)(2,1)} %qkv_hbm.1, bf16[512,512]{1,0:T(8,128)(2,1)} %proj_hbm.1, bf16[512,2048]{1,0:T(8,128)(2,1)} %fc1_hbm.1, bf16[2048,512]{1,0:T(8,128)(2,1)} %fc2_hbm.1, bf16[2048,1024]{1,0:T(8,128)(2,1)} %merge_hbm.1, s32[48]{0:T(128)} %band_ids.1), custom_call_target="tpu_custom_call" | custom-call | tf_op jit(solution)/shard_map/layer/pallas_call | solution.py:350
  56.8 1.9 %copy.9 = bf16[4,3,64,384]{3,2,1,0:T(8,128)(2,1)} copy(bf16[4,3,64,384]{3,2,1,0:T(8,128)(2,1)} %layer.1) | data formatting | bytes 1179648

commit v4 on v3

v4 whole, which is shorter than its diff:
```python
import jax
import jax.numpy as jnp
from jax import lax
from jax.experimental import pallas as pl
from jax.experimental.pallas import tpu as pltpu
from jax.sharding import PartitionSpec as P

MESH = pl.DeviceIdType.MESH
BF16 = jnp.bfloat16
F32 = jnp.float32
PEERS = 16
LAT = 8
WIDTH = 512
NEVER = -1e30


def unit_row(half, unit):
    return unit if half == 0 else 5 - unit


def split(index, size):
    whole = jnp.floor((index + 0.5) * (1.0 / size))
    return whole, index - whole * size


def one_hot(picks, width):
    lane = lax.broadcasted_iota(jnp.int32, picks.shape, 1).astype(F32)
    tiles = [jnp.where(lane + at == picks, 1.0, 0.0) for at in range(0, width, 128)]
    return jnp.concatenate(tiles, axis=1)[:, 0:width].astype(BF16)


def index_of(rows):
    return lax.broadcasted_iota(jnp.int32, (rows, 128), 0).astype(F32)


def edge_picks():
    index = index_of(80)
    half, rest = split(index, 36)
    unit, rest = split(rest, 12)
    level, col = split(rest, 6)
    row = unit + half * (5 - 2 * unit)
    return jnp.where(index < 72, (level * 6 + row) * 48 + col, -1.0)


def window_picks():
    half, rest = split(index_of(576), 288)
    win, rest = split(rest, 72)
    unit, rest = split(rest, 24)
    level, col = split(rest, 12)
    row = unit + half * (5 - 2 * unit)
    at = win * 12 + 6 + col
    return jnp.where(at < 48, (level * 6 + row) * 48 + at, -1.0)


def window_edge_picks():
    group, col = split(index_of(144), 12)
    return jnp.where(col > 5.5, group * 6 + col - 6, -1.0)


def back_picks():
    group, col = split(index_of(48), 6)
    return group * 12 + 6 + col


def merge_picks():
    parity, rest = split(index_of(384), 96)
    col_parity, row_parity = split(parity, 2)
    s, rest = split(rest, 48)
    t, b = split(rest, 24)
    col = 2 * b + col_parity
    win, at = split(col - 6, 12)
    here = col > 5.5
    half = row_parity
    middle = jnp.where(here, s * 192 + (half * 4 + win) * 24 + t * 12 + at, -1.0)
    middle_edge = jnp.where(here, -1.0, ((s * 2 + half) * 2 + t) * 6 + col)
    unit = row_parity + t * (1 - 2 * row_parity)
    outer = jnp.where(here, (t * 4 + win) * 48 + unit * 24 + s * 12 + at, -1.0)
    outer_edge = jnp.where(here, -1.0, ((t * 2 + unit) * 2 + s) * 6 + col)
    return (middle, middle_edge), (outer, outer_edge)


def dot(a, b):
    return jnp.dot(a, b, preferred_element_type=F32)


def layer_norm(values):
    average = jnp.mean(values, axis=-1, keepdims=True)
    centred = values - average
    spread = jnp.mean(centred * centred, axis=-1, keepdims=True)
    return centred * lax.rsqrt(spread + 1e-05)


def attend(block, query_at, bias):
    head = lax.broadcasted_iota(jnp.int32, (48, 256), 1) // 64
    result = []
    for quad in range(2):
        at = 256 * quad
        query = block[pl.ds(query_at, 48), pl.ds(at, 256)] * 0.125
        query = jnp.concatenate([jnp.where(head == h, query, 0.0) for h in range(4)], axis=0)
        key = block[:, pl.ds(512 + at, 256)].astype(BF16)
        value = block[:, pl.ds(1024 + at, 256)].astype(BF16)
        scores = lax.dot_general(
            query.astype(BF16), key, (((1,), (1,)), ((), ())), preferred_element_type=F32
        )
        scores = scores + bias
        weights = jnp.exp(scores - jnp.max(scores, axis=-1, keepdims=True))
        total = jnp.sum(weights, axis=-1, keepdims=True)
        mixed = dot(weights.astype(BF16), value) / total
        picked = mixed[0:48]
        for h in range(1, 4):
            picked = jnp.where(head == h, mixed[48 * h : 48 * h + 48], picked)
        result.append(picked)
    return result


def band_biases(band_ids, lat, bias_own, bias_rim):
    seen, final = [], []
    for half in range(2):
        units = [unit_row(half, u) for u in range(3)] + ([-1, -2, -3] if half == 0 else [6, 7, 8])
        band = [band_ids[lax.rem(lat * 6 + u + 48, 48)] for u in units]

        def band_of(shape, dim):
            unit = lax.broadcasted_iota(jnp.int32, shape, dim) // 24
            held = jnp.full(shape, -1, jnp.int32)
            for u in range(5):
                held = jnp.where(unit == u, band[u], held)
            return held

        bias = jnp.where(band_of((96, 128), 0) == band_of((96, 128), 1), 0.0, NEVER)
        near = lax.broadcasted_iota(jnp.int32, (48, 128), 1) < 96
        for head in range(4):
            bias_own[half, pl.ds(48 * head, 48), :] = bias[0:48]
            bias_rim[half, pl.ds(48 * head, 48), :] = jnp.where(near, bias[48:96], NEVER)
        seen.append(jnp.full((1, WIDTH), band[2], jnp.int32) == band[3])
        final.append(jnp.full((1, WIDTH), band[0], jnp.int32) == band[5])
    return seen, final


def finish_chunk(restored, fc1, fc2, merge):
    base = restored.astype(F32)
    normed = layer_norm(base).astype(BF16)
    hidden = []
    for i in range(4):
        pre = dot(normed, fc1[:, pl.ds(512 * i, 512)])
        hidden.append((0.5 * pre * (1.0 + lax.erf(pre * 0.7071067811865476))).astype(BF16))
    done = (base + dot(jnp.concatenate(hidden, axis=1), fc2[...])).astype(BF16).astype(F32)
    pieces = [done[96 * i : 96 * i + 96] for i in range(4)]
    average = sum(jnp.sum(p, axis=-1, keepdims=True) for p in pieces) / 2048
    pieces = [p - average for p in pieces]
    spread = sum(jnp.sum(p * p, axis=-1, keepdims=True) for p in pieces) / 2048
    scale = lax.rsqrt(spread + 1e-05)
    return dot(jnp.concatenate([(p * scale).astype(BF16) for p in pieces], axis=1), merge[...])


def pack_chunk(merged, send):
    low = lax.broadcasted_iota(jnp.int32, (48, 128), 1) < 64
    for j in range(8):
        one = merged[0:48, 128 * j : 128 * j + 128]
        two = merged[48:96, 128 * j : 128 * j + 128]
        send[2 * j] = jnp.where(low, one, pltpu.roll(two, 64, 1)).astype(BF16)
        send[2 * j + 1] = jnp.where(low, pltpu.roll(one, 64, 1), two).astype(BF16)


def unpack_chunk(got, out, chunk):
    for t in range(2):
        lines = jnp.concatenate(
            [got[s].astype(F32)[24 * t : 24 * t + 24, :] for s in range(PEERS)], axis=0
        )
        turned = lines.T.astype(BF16)
        if chunk == 0:
            out[t, 1] = turned[0:64, :]
            out[2 + t, 1] = turned[64:128, :]
        else:
            out[2 * chunk - 2, 2 * t] = turned[0:64, :]
            out[2 * chunk - 1, 2 * t] = turned[64:128, :]


def kernel(
    tokens_hbm, qkv_hbm, proj_hbm, fc1_hbm, fc2_hbm, merge_hbm, band_ids,
    out,
    tokens, first, window, window_edge, back, middle, middle_edge, outer, outer_edge,
    qkv, proj, fc1, fc2, merge,
    edge_out, edge_in, placed, rim_out, rim_in, far_out, far_in, packed,
    middle_mixed, rim_mixed, outer_mixed, back_out, back_in, send, got, bias_own, bias_rim,
    token_sem, load_sem, edge_sem, rim_sem, far_sem, back_sem, send_sem, recv_sem, own_sem,
):
    sources = [qkv_hbm, proj_hbm, fc1_hbm, fc2_hbm, merge_hbm]
    places = [qkv, proj, fc1, fc2, merge]
    token_loads = [
        pltpu.make_async_copy(tokens_hbm.at[pl.ds(576 * g, 576)], tokens.at[g], token_sem.at[g])
        for g in range(2)
    ]
    loads = [
        pltpu.make_async_copy(src, dst, load_sem.at[i])
        for i, (src, dst) in enumerate(zip(sources, places))
    ]
    for load in token_loads + loads[:1]:
        load.start()

    lat = lax.axis_index("lat")
    lon = lax.axis_index("lon")
    up = {"lat": lax.rem(lat + LAT - 1, LAT)}
    down = {"lat": lax.rem(lat + 1, LAT)}
    west = {"lon": lax.rem(lon + PEERS - 1, PEERS)}
    east = {"lon": lax.rem(lon + 1, PEERS)}
    barrier = pltpu.get_barrier_semaphore()
    for to in (up, down):
        pl.semaphore_signal(barrier, inc=1, device_id=to, device_id_type=MESH)
    for d in range(1, PEERS):
        pl.semaphore_signal(
            barrier, inc=1, device_id={"lon": lax.rem(lon + d, PEERS)}, device_id_type=MESH
        )
    first[...] = one_hot(edge_picks(), 576)
    window[...] = one_hot(window_picks(), 576)
    window_edge[...] = one_hot(window_edge_picks(), 80)

    def remote(src, dst, sems, where, to):
        copy = pltpu.make_async_remote_copy(
            src_ref=src, dst_ref=dst, send_sem=sems.at[(0,) + where], recv_sem=sems.at[(1,) + where],
            device_id=to, device_id_type=MESH,
        )
        copy.start()
        return copy

    def send_rim(g, part):
        rows = (pl.ds(0, 64), pl.ds(64, 32))[part]
        return [
            remote(
                rim_out.at[g, half, rows], rim_in.at[g, 1 - half, rows],
                rim_sem, (g, half, part), (up, down)[half],
            )
            for half in range(2)
        ]

    def fill_rim(g, part):
        for half in range(2):
            at = 288 * half
            if part == 0:
                rows = [(at, 24), (at + 72, 24), (at + 144, 16)]
            else:
                rows = [(at + 160, 8), (at + 216, 24)]
            rim_out[g, half, pl.ds(64 * part, 64 - 32 * part), :] = jnp.concatenate(
                [placed[g, pl.ds(start, size), :] for start, size in rows], axis=0
            ).astype(BF16)

    def add_edge(g):
        edges[g].wait_recv()
        fresh = dot(window_edge[...], edge_in[g])
        for half in range(2):
            rows = pl.ds(288 * half + 216, 72)
            placed[g, rows, :] = placed[g, rows, :] + fresh[72 * half : 72 * half + 72]

    def own_qkv(blocks):
        values = jnp.concatenate([placed[g, pl.ds(72 * k, 72 * n), :] for g, k, n in blocks], axis=0)
        normed = layer_norm(values).astype(BF16)
        for part in range(3):
            cols = pl.ds(512 * part, 512)
            result = dot(normed, qkv[:, cols])
            at = 0
            for g, k, n in blocks:
                for i in range(n):
                    packed[g, k + i, pl.ds(0, 72), cols] = result[at : at + 72]
                    at += 72

    for g in range(2):
        token_loads[g].wait()
        edge_out[g] = dot(first[...], tokens[g]).astype(BF16)
    placed[0] = dot(window[...], tokens[0])
    fill_rim(0, 0)
    pl.semaphore_wait(barrier, PEERS + 1)
    edges = [remote(edge_out.at[g], edge_in.at[g], edge_sem, (g,), west) for g in range(2)]
    rims = [send_rim(0, 0), []]
    for load in loads[1:]:
        load.start()
    placed[1] = dot(window[...], tokens[1])
    fill_rim(1, 0)
    loads[0].wait()
    own_qkv([(0, 0, 3), (0, 4, 3)])
    add_edge(0)
    fill_rim(0, 1)
    rims[0] += send_rim(0, 1)
    rims[1] += send_rim(1, 0)
    add_edge(1)
    fill_rim(1, 1)
    rims[1] += send_rim(1, 1)
    own_qkv([(0, 3, 1), (0, 7, 1), (1, 3, 1), (1, 7, 1)])
    own_qkv([(1, 0, 3), (1, 4, 3)])
    for g in range(2):
        for k in range(8):
            packed[g, k, pl.ds(96, 32), :] = jnp.zeros((32, 1536), F32)
    edge_seen, edge_final = band_biases(band_ids, lat, bias_own, bias_rim)
    inner_picks, outer_picks = merge_picks()
    middle[...] = one_hot(inner_picks[0], 384)
    middle_edge[...] = one_hot(inner_picks[1], 48)
    outer[...] = one_hot(outer_picks[0], 384)
    outer_edge[...] = one_hot(outer_picks[1], 48)
    back[...] = one_hot(back_picks(), 96)
    fars = []
    for g in range(2):
        for copy in rims[g]:
            copy.wait_recv()
        rim = rim_in[g].reshape(192, WIDTH)
        normed = layer_norm(rim.astype(F32)).astype(BF16)
        for part in range(3):
            cols = pl.ds(512 * part, 512)
            result = dot(normed, qkv[:, cols])
            for k in range(8):
                packed[g, k, pl.ds(72, 24), cols] = result[24 * k : 24 * k + 24]
        for k in range(8):
            parts = attend(packed.at[g, k], 48, bias_rim[k // 4])
            for quad in range(2):
                cols = pl.ds(256 * quad, 256)
                middle_mixed[pl.ds(192 * g + 24 * k, 24), cols] = parts[quad][0:24]
                rim_mixed[g, pl.ds(24 * k, 24), cols] = parts[quad][24:48]
        for half in range(2):
            second = jnp.concatenate(
                [placed[g, pl.ds(288 * half + 72 * w + 24, 24), :] for w in range(4)], axis=0
            )
            far_out[g, half] = jnp.where(
                edge_seen[half], rim_mixed[g, pl.ds(96 * half, 96), :], second
            ).astype(BF16)
            fars.append(
                remote(far_out.at[g, half], far_in.at[g, 1 - half], far_sem, (g, half), (up, down)[half])
            )
    copies = []
    backs = []

    def project(mixed, own, chunk):
        fresh = own + dot(mixed.astype(BF16), proj[...])
        if chunk == 0:
            rim = [fresh[192 * g + 24 * k : 192 * g + 24 * k + 24] for g in range(2) for k in (3, 7)]
        else:
            rim = [fresh[48 * k : 48 * k + 48] for k in (3, 7)]
        back_out[chunk] = dot(back[...], jnp.concatenate(rim, axis=0).astype(BF16)).astype(BF16)
        backs.append(remote(back_out.at[chunk], back_in.at[chunk], back_sem, (chunk,), east))
        return fresh.astype(BF16)

    def finish(updated, chunk):
        order, order_edge = (middle, middle_edge) if chunk == 0 else (outer, outer_edge)
        inner = dot(order[...], updated)
        backs[chunk].wait_recv()
        restored = (inner + dot(order_edge[...], back_in[chunk])).astype(BF16)
        pack_chunk(finish_chunk(restored, fc1, fc2, merge), send.at[chunk])
        group = []
        for d in range(1, PEERS):
            to = lax.rem(lon + d, PEERS)
            copy = pltpu.make_async_remote_copy(
                src_ref=send.at[chunk, to], dst_ref=got.at[chunk, lon],
                send_sem=send_sem.at[chunk, d], recv_sem=recv_sem.at[chunk, d],
                device_id={"lon": to}, device_id_type=MESH,
            )
            copy.start()
            group.append(copy)
        copy = pltpu.make_async_copy(send.at[chunk, lon], got.at[chunk, lon], own_sem.at[chunk])
        copy.start()
        copies.append(group + [copy])

    def collect(chunk):
        for copy in copies[chunk]:
            copy.wait()
        unpack_chunk(got.at[chunk], out, chunk)

    loads[1].wait()
    own = jnp.concatenate(
        [placed[g, pl.ds(72 * k + 48, 24), :] for g in range(2) for k in range(8)], axis=0
    )
    updates = [project(middle_mixed[...], own, 0)]
    for load in loads[2:]:
        load.wait()
    for g in range(2):
        for half in range(2):
            fars[2 * g + half].wait_recv()
        far = far_in[g].reshape(192, WIDTH)
        normed = layer_norm(far.astype(F32)).astype(BF16)
        for part in range(1, 3):
            cols = pl.ds(512 * part, 512)
            result = dot(normed, qkv[:, cols])
            for k in range(8):
                packed[g, k, pl.ds(96, 24), cols] = result[24 * k : 24 * k + 24]
        for k in range(8):
            parts = attend(packed.at[g, k], 0, bias_own[k // 4])
            for quad in range(2):
                outer_mixed[pl.ds(48 * k, 48), pl.ds(256 * quad, 256)] = parts[quad]
        for half in range(2):
            final = far_in[g, half].astype(F32)
            for w in range(4):
                rows = pl.ds(192 * half + 48 * w, 24)
                outer_mixed[rows, :] = jnp.where(
                    edge_final[half], final[24 * w : 24 * w + 24], outer_mixed[rows, :]
                )
        own = jnp.concatenate([placed[g, pl.ds(72 * k, 48), :] for k in range(8)], axis=0)
        updates.append(project(outer_mixed[...], own, g + 1))
        if g == 0:
            finish(updates[0], 0)
    finish(updates[1], 1)
    collect(0)
    finish(updates[2], 2)
    collect(1)
    collect(2)
    for copy in edges + rims[0] + rims[1] + fars + backs:
        copy.wait_send()


def body(tokens, band_ids, qkv_weight, proj_weight, fc1_weight, fc2_weight, merge_weight):
    hbm = pl.BlockSpec(memory_space=pl.ANY)
    vmem = pl.BlockSpec(memory_space=pltpu.VMEM)
    dma = pltpu.SemaphoreType.DMA
    return pl.pallas_call(
        kernel,
        out_shape=jax.ShapeDtypeStruct((4, 3, 64, 384), BF16),
        in_specs=[hbm] * 6 + [pl.BlockSpec(memory_space=pltpu.SMEM)],
        out_specs=vmem,
        scratch_shapes=[
            pltpu.VMEM((2, 576, WIDTH), BF16),
            pltpu.VMEM((80, 576), BF16),
            pltpu.VMEM((576, 576), BF16),
            pltpu.VMEM((144, 80), BF16),
            pltpu.VMEM((48, 96), BF16),
            pltpu.VMEM((384, 384), BF16),
            pltpu.VMEM((384, 48), BF16),
            pltpu.VMEM((384, 384), BF16),
            pltpu.VMEM((384, 48), BF16),
            pltpu.VMEM((512, 1536), BF16),
            pltpu.VMEM((512, 512), BF16),
            pltpu.VMEM((512, 2048), BF16),
            pltpu.VMEM((2048, 512), BF16),
            pltpu.VMEM((2048, 1024), BF16),
            pltpu.VMEM((2, 80, WIDTH), BF16),
            pltpu.VMEM((2, 80, WIDTH), BF16),
            pltpu.VMEM((2, 576, WIDTH), F32),
            pltpu.VMEM((2, 2, 96, WIDTH), BF16),
            pltpu.VMEM((2, 2, 96, WIDTH), BF16),
            pltpu.VMEM((2, 2, 96, WIDTH), BF16),
            pltpu.VMEM((2, 2, 96, WIDTH), BF16),
            pltpu.VMEM((2, 8, 128, 1536), F32),
            pltpu.VMEM((384, WIDTH), F32),
            pltpu.VMEM((2, 192, WIDTH), F32),
            pltpu.VMEM((384, WIDTH), F32),
            pltpu.VMEM((3, 48, WIDTH), BF16),
            pltpu.VMEM((3, 48, WIDTH), BF16),
            pltpu.VMEM((3, PEERS, 48, 128), BF16),
            pltpu.VMEM((3, PEERS, 48, 128), BF16),
            pltpu.VMEM((2, 192, 128), F32),
            pltpu.VMEM((2, 192, 128), F32),
            dma((2,)),
            dma((5,)),
            dma((2, 2)),
            dma((2, 2, 2, 2)),
            dma((2, 2, 2)),
            dma((2, 3)),
            dma((3, PEERS)),
            dma((3, PEERS)),
            dma((3,)),
        ],
        compiler_params=pltpu.CompilerParams(
            collective_id=0, has_side_effects=True, vmem_limit_bytes=56 * 1024 * 1024
        ),
        name="layer",
    )(
        tokens.reshape(4 * 6 * 48, WIDTH),
        qkv_weight, proj_weight, fc1_weight, fc2_weight, merge_weight, band_ids,
    )


def solution(mesh):
    placed = (P(None, "lat", "lon", None), P(), P(), P(), P(), P(), P())
    return jax.shard_map(
        body, mesh=mesh, in_specs=placed, out_specs=P(None, "lat", "lon", None), check_vma=False
    )
```

time: 58.9 us -> 54.2 us (0.920)
  Pallas kernels: 56.8 us -> 52.1 us
    pallas_call x1, Pallas kernels: 56.8 us -> 52.1 us  [body(): pl.pallas_call(kernel, out_shape=jax.ShapeDtypeStruct((4, 3, 64, 384), BF...]
where the time goes in v4:
time: 54.2 us; the launch traced here: 54 us
  Pallas kernels  52.1 us (96%)
  local copies, waits for them, and re-layouts  1.94 us (4%)
    pallas_call x1, Pallas kernels, body(): pl.pallas_call(kernel, out_shape=jax.ShapeDtypeStruct((4, 3, 64, 384), BF...  52.1 us
    unnamed x1, local copies, waits for them, and re-layouts  1.94 us

profile of v4, /device:TPU:1, one launch (start us, length us, event | category | flops | bytes accessed | tf_op | source)
XLA Modules:
  0.0 54.0 jit_solution(11710901221676124631)
XLA Ops:
  0.0 52.1 %layer.1 = bf16[4,3,64,384]{3,2,1,0:T(8,128)(2,1)} custom-call(bf16[1152,512]{1,0:T(8,128)(2,1)} %bitcast.1, bf16[512,1536]{1,0:T(8,128)(2,1)} %qkv_hbm.1, bf16[512,512]{1,0:T(8,128)(2,1)} %proj_hbm.1, bf16[512,2048]{1,0:T(8,128)(2,1)} %fc1_hbm.1, bf16[2048,512]{1,0:T(8,128)(2,1)} %fc2_hbm.1, bf16[2048,1024]{1,0:T(8,128)(2,1)} %merge_hbm.1, s32[48]{0:T(128)} %band_ids.1), custom_call_target="tpu_custom_call" | custom-call | tf_op jit(solution)/shard_map/layer/pallas_call | solution.py:408
  52.1 1.9 %copy.9 = bf16[4,3,64,384]{3,2,1,0:T(8,128)(2,1)} copy(bf16[4,3,64,384]{3,2,1,0:T(8,128)(2,1)} %layer.1) | data formatting | bytes 1179648

commit v5 on v4

--- a/solution.py
+++ b/solution.py
@@ -177,11 +177,11 @@
 
 def kernel(
     tokens_hbm, qkv_hbm, proj_hbm, fc1_hbm, fc2_hbm, merge_hbm, band_ids,
-    out,
+    got,
     tokens, first, window, window_edge, back, middle, middle_edge, outer, outer_edge,
     qkv, proj, fc1, fc2, merge,
     edge_out, edge_in, placed, rim_out, rim_in, far_out, far_in, packed,
-    middle_mixed, rim_mixed, outer_mixed, back_out, back_in, send, got, bias_own, bias_rim,
+    middle_mixed, rim_mixed, outer_mixed, back_out, back_in, send, bias_own, bias_rim,
     token_sem, load_sem, edge_sem, rim_sem, far_sem, back_sem, send_sem, recv_sem, own_sem,
 ):
     sources = [qkv_hbm, proj_hbm, fc1_hbm, fc2_hbm, merge_hbm]
@@ -355,11 +355,6 @@
         copy.start()
         copies.append(group + [copy])
 
-    def collect(chunk):
-        for copy in copies[chunk]:
-            copy.wait()
-        unpack_chunk(got.at[chunk], out, chunk)
-
     loads[1].wait()
     own = jnp.concatenate(
         [placed[g, pl.ds(72 * k + 48, 24), :] for g in range(2) for k in range(8)], axis=0
@@ -393,23 +388,28 @@
         if g == 0:
             finish(updates[0], 0)
     finish(updates[1], 1)
-    collect(0)
     finish(updates[2], 2)
-    collect(1)
-    collect(2)
+    for group in copies:
+        for copy in group:
+            copy.wait()
     for copy in edges + rims[0] + rims[1] + fars + backs:
         copy.wait_send()
+
+
+def unpack_kernel(got, out):
+    for chunk in range(3):
+        unpack_chunk(got.at[chunk], out, chunk)
 
 
 def body(tokens, band_ids, qkv_weight, proj_weight, fc1_weight, fc2_weight, merge_weight):
     hbm = pl.BlockSpec(memory_space=pl.ANY)
     vmem = pl.BlockSpec(memory_space=pltpu.VMEM)
     dma = pltpu.SemaphoreType.DMA
-    return pl.pallas_call(
+    got = pl.pallas_call(
         kernel,
-        out_shape=jax.ShapeDtypeStruct((4, 3, 64, 384), BF16),
+        out_shape=jax.ShapeDtypeStruct((3, PEERS, 48, 128), BF16),
         in_specs=[hbm] * 6 + [pl.BlockSpec(memory_space=pltpu.SMEM)],
-        out_specs=vmem,
+        out_specs=hbm,
         scratch_shapes=[
             pltpu.VMEM((2, 576, WIDTH), BF16),
             pltpu.VMEM((80, 576), BF16),
@@ -439,7 +439,6 @@
             pltpu.VMEM((3, 48, WIDTH), BF16),
             pltpu.VMEM((3, 48, WIDTH), BF16),
             pltpu.VMEM((3, PEERS, 48, 128), BF16),
-            pltpu.VMEM((3, PEERS, 48, 128), BF16),
             pltpu.VMEM((2, 192, 128), F32),
             pltpu.VMEM((2, 192, 128), F32),
             dma((2,)),
@@ -460,6 +459,13 @@
         tokens.reshape(4 * 6 * 48, WIDTH),
         qkv_weight, proj_weight, fc1_weight, fc2_weight, merge_weight, band_ids,
     )
+    return pl.pallas_call(
+        unpack_kernel,
+        out_shape=jax.ShapeDtypeStruct((4, 3, 64, 384), BF16),
+        in_specs=[vmem],
+        out_specs=vmem,
+        name="unpack",
+    )(got)
 
 
 def solution(mesh):

time: 54.2 us -> 53.3 us (0.983)
  local copies, waits for them, and re-layouts: 1.94 us -> 0 us
  Pallas kernels: 52.1 us -> 53.1 us
    unnamed x1 -> x0, local copies, waits for them, and re-layouts: 1.94 us -> none
    pallas_call x1 -> x2, Pallas kernels: 52.1 us -> 53.1 us  [the longest x1 51 us: body(): pl.pallas_call(kernel, out_shape=jax.ShapeDtypeStruct((3, PEERS, 48, 128)...]
where the time goes in v5:
time: 53.3 us; the launch traced here: 53.1 us
  Pallas kernels  53.1 us (100%)
    pallas_call x1, Pallas kernels, body(): pl.pallas_call(kernel, out_shape=jax.ShapeDtypeStruct((3, PEERS, 48, 128)...  51 us
    pallas_call x1, Pallas kernels, body(): pl.pallas_call(unpack_kernel, out_shape=jax.ShapeDtypeStruct((4, 3, 64, 3...  2.12 us

profile of v5, /device:TPU:1, one launch (start us, length us, event | category | flops | bytes accessed | tf_op | source)
XLA Modules:
  0.0 53.1 jit_solution(9196163398943781346)
XLA Ops:
  0.0 51.0 %layer.1.got = bf16[3,16,48,128]{3,2,1,0:T(8,128)(2,1)} custom-call(bf16[1152,512]{1,0:T(8,128)(2,1)} %bitcast.1, bf16[512,1536]{1,0:T(8,128)(2,1)} %qkv_hbm.1, bf16[512,512]{1,0:T(8,128)(2,1)} %proj_hbm.1, bf16[512,2048]{1,0:T(8,128)(2,1)} %fc1_hbm.1, bf16[2048,512]{1,0:T(8,128)(2,1)} %fc2_hbm.1, bf16[2048,1024]{1,0:T(8,128)(2,1)} %merge_hbm.1, s32[48]{0:T(128)} %band_ids.1), custom_call_target="tpu_custom_call" | custom-call | tf_op jit(solution)/shard_map/layer/pallas_call | solution.py:408
  51.0 2.1 %unpack.1 = bf16[4,3,64,384]{3,2,1,0:T(8,128)(2,1)} custom-call(bf16[3,16,48,128]{3,2,1,0:T(8,128)(2,1)} %layer.1.got), custom_call_target="tpu_custom_call" | custom-call | tf_op jit(solution)/shard_map/unpack/pallas_call | solution.py:462

commit v6 on v5

--- a/solution.py
+++ b/solution.py
@@ -12,6 +12,7 @@
 LAT = 8
 WIDTH = 512
 NEVER = -1e30
+FAR_FIRST = sorted(range(1, PEERS), key=lambda d: -min(d, PEERS - d))
 
 
 def unit_row(half, unit):
@@ -182,7 +183,7 @@
     qkv, proj, fc1, fc2, merge,
     edge_out, edge_in, placed, rim_out, rim_in, far_out, far_in, packed,
     middle_mixed, rim_mixed, outer_mixed, back_out, back_in, send, bias_own, bias_rim,
-    token_sem, load_sem, edge_sem, rim_sem, far_sem, back_sem, send_sem, recv_sem, own_sem,
+    token_sem, load_sem, edge_sem, rim_sem, far_sem, back_sem, send_sem, recv_sem,
 ):
     sources = [qkv_hbm, proj_hbm, fc1_hbm, fc2_hbm, merge_hbm]
     places = [qkv, proj, fc1, fc2, merge]
@@ -322,7 +323,6 @@
             fars.append(
                 remote(far_out.at[g, half], far_in.at[g, 1 - half], far_sem, (g, half), (up, down)[half])
             )
-    copies = []
     backs = []
 
     def project(mixed, own, chunk):
@@ -341,19 +341,15 @@
         backs[chunk].wait_recv()
         restored = (inner + dot(order_edge[...], back_in[chunk])).astype(BF16)
         pack_chunk(finish_chunk(restored, fc1, fc2, merge), send.at[chunk])
-        group = []
-        for d in range(1, PEERS):
+        for d in FAR_FIRST:
             to = lax.rem(lon + d, PEERS)
             copy = pltpu.make_async_remote_copy(
                 src_ref=send.at[chunk, to], dst_ref=got.at[chunk, lon],
-                send_sem=send_sem.at[chunk, d], recv_sem=recv_sem.at[chunk, d],
+                send_sem=send_sem.at[chunk], recv_sem=recv_sem.at[chunk],
                 device_id={"lon": to}, device_id_type=MESH,
             )
             copy.start()
-            group.append(copy)
-        copy = pltpu.make_async_copy(send.at[chunk, lon], got.at[chunk, lon], own_sem.at[chunk])
-        copy.start()
-        copies.append(group + [copy])
+        pltpu.make_async_copy(send.at[chunk, lon], got.at[chunk, lon], recv_sem.at[chunk]).start()
 
     loads[1].wait()
     own = jnp.concatenate(
@@ -389,9 +385,10 @@
             finish(updates[0], 0)
     finish(updates[1], 1)
     finish(updates[2], 2)
-    for group in copies:
-        for copy in group:
-            copy.wait()
+    for chunk in range(3):
+        sent = send.at[chunk, pl.ds(0, PEERS - 1)]
+        pltpu.make_async_copy(sent, sent, send_sem.at[chunk]).wait()
+        pltpu.make_async_copy(got.at[chunk], got.at[chunk], recv_sem.at[chunk]).wait()
     for copy in edges + rims[0] + rims[1] + fars + backs:
         copy.wait_send()
 
@@ -447,8 +444,7 @@
             dma((2, 2, 2, 2)),
             dma((2, 2, 2)),
             dma((2, 3)),
-            dma((3, PEERS)),
-            dma((3, PEERS)),
+            dma((3,)),
             dma((3,)),
         ],
         compiler_params=pltpu.CompilerParams(

time: 53.3 us -> 51.8 us (0.972)
  Pallas kernels: 53.1 us -> 51.6 us
    pallas_call x1, Pallas kernels: 51 us -> 49.5 us  [body(): pl.pallas_call(kernel, out_shape=jax.ShapeDtypeStruct((3, PEERS, 48, 128)...]
where the time goes in v6:
time: 51.8 us; the launch traced here: 51.7 us
  Pallas kernels  51.6 us (100%)
    pallas_call x1, Pallas kernels, body(): pl.pallas_call(kernel, out_shape=jax.ShapeDtypeStruct((3, PEERS, 48, 128)...  49.5 us
    pallas_call x1, Pallas kernels, body(): pl.pallas_call(unpack_kernel, out_shape=jax.ShapeDtypeStruct((4, 3, 64, 3...  2.12 us

profile of v6, /device:TPU:1, one launch (start us, length us, event | category | flops | bytes accessed | tf_op | source)
XLA Modules:
  0.0 51.7 jit_solution(10370429278915315910)
XLA Ops:
  0.0 49.5 %layer.1.got = bf16[3,16,48,128]{3,2,1,0:T(8,128)(2,1)} custom-call(bf16[1152,512]{1,0:T(8,128)(2,1)} %bitcast.1, bf16[512,1536]{1,0:T(8,128)(2,1)} %qkv_hbm.1, bf16[512,512]{1,0:T(8,128)(2,1)} %proj_hbm.1, bf16[512,2048]{1,0:T(8,128)(2,1)} %fc1_hbm.1, bf16[2048,512]{1,0:T(8,128)(2,1)} %fc2_hbm.1, bf16[2048,1024]{1,0:T(8,128)(2,1)} %merge_hbm.1, s32[48]{0:T(128)} %band_ids.1), custom_call_target="tpu_custom_call" | custom-call | tf_op jit(solution)/shard_map/layer/pallas_call | solution.py:405
  49.5 2.1 %unpack.1 = bf16[4,3,64,384]{3,2,1,0:T(8,128)(2,1)} custom-call(bf16[3,16,48,128]{3,2,1,0:T(8,128)(2,1)} %layer.1.got), custom_call_target="tpu_custom_call" | custom-call | tf_op jit(solution)/shard_map/unpack/pallas_call | solution.py:458

commit v7 on v6

--- a/solution.py
+++ b/solution.py
@@ -163,11 +163,17 @@
 
 
 def unpack_chunk(got, out, chunk):
+    shape = (128, 128)
+    same = jnp.where(
+        lax.broadcasted_iota(jnp.int32, shape, 0) == lax.broadcasted_iota(jnp.int32, shape, 1), 1.0, 0.0
+    ).astype(BF16)
     for t in range(2):
         lines = jnp.concatenate(
             [got[s].astype(F32)[24 * t : 24 * t + 24, :] for s in range(PEERS)], axis=0
         )
-        turned = lines.T.astype(BF16)
+        turned = lax.dot_general(
+            same, lines.astype(BF16), (((1,), (1,)), ((), ())), preferred_element_type=F32
+        ).astype(BF16)
         if chunk == 0:
             out[t, 1] = turned[0:64, :]
             out[2 + t, 1] = turned[64:128, :]
@@ -385,12 +391,12 @@
             finish(updates[0], 0)
     finish(updates[1], 1)
     finish(updates[2], 2)
+    for copy in edges + rims[0] + rims[1] + fars + backs:
+        copy.wait_send()
     for chunk in range(3):
         sent = send.at[chunk, pl.ds(0, PEERS - 1)]
         pltpu.make_async_copy(sent, sent, send_sem.at[chunk]).wait()
         pltpu.make_async_copy(got.at[chunk], got.at[chunk], recv_sem.at[chunk]).wait()
-    for copy in edges + rims[0] + rims[1] + fars + backs:
-        copy.wait_send()
 
 
 def unpack_kernel(got, out):

time: 51.8 us -> 52 us (level)
  no operation moved by 1% of the time
where the time goes in v7:
time: 52 us; the launch traced here: 51.8 us
  Pallas kernels  51.8 us (100%)
    pallas_call x1, Pallas kernels, body(): pl.pallas_call(kernel, out_shape=jax.ShapeDtypeStruct((3, PEERS, 48, 128)...  49.5 us
    pallas_call x1, Pallas kernels, body(): pl.pallas_call(unpack_kernel, out_shape=jax.ShapeDtypeStruct((4, 3, 64, 3...  2.27 us

profile of v7, /device:TPU:1, one launch (start us, length us, event | category | flops | bytes accessed | tf_op | source)
XLA Modules:
  0.0 51.8 jit_solution(12358472020406055339)
XLA Ops:
  0.0 49.5 %layer.1.got = bf16[3,16,48,128]{3,2,1,0:T(8,128)(2,1)} custom-call(bf16[1152,512]{1,0:T(8,128)(2,1)} %bitcast.1, bf16[512,1536]{1,0:T(8,128)(2,1)} %qkv_hbm.1, bf16[512,512]{1,0:T(8,128)(2,1)} %proj_hbm.1, bf16[512,2048]{1,0:T(8,128)(2,1)} %fc1_hbm.1, bf16[2048,512]{1,0:T(8,128)(2,1)} %fc2_hbm.1, bf16[2048,1024]{1,0:T(8,128)(2,1)} %merge_hbm.1, s32[48]{0:T(128)} %band_ids.1), custom_call_target="tpu_custom_call" | custom-call | tf_op jit(solution)/shard_map/layer/pallas_call | solution.py:411
  49.5 2.3 %unpack.1 = bf16[4,3,64,384]{3,2,1,0:T(8,128)(2,1)} custom-call(bf16[3,16,48,128]{3,2,1,0:T(8,128)(2,1)} %layer.1.got), custom_call_target="tpu_custom_call" | custom-call | tf_op jit(solution)/shard_map/unpack/pallas_call | solution.py:464
